TPU v7x, 128 devices: a whole 4x4x4 slice. The times are simulated.
128 devices in a mesh: dp: 2 (over z_hi), branch: 8 (over y, z_lo), tensor: 8 (over x, core).
Axes of the slice: x: 4, y: 4, z: 4 (z_hi: 2, z_lo: 2; z = z_hi * 2 + z_lo), core: 2. Of those that a mesh axis runs over, the one named last changes fastest.
Arguments:
- queries: bfloat16 [2, 2048, 8192], P('dp', 'branch', 'tensor'), may hold values from -8 to 8
- prefix_keys: bfloat16 [2, 2048, 1024], P('dp', 'branch', 'tensor'), may hold values from -8 to 8
- prefix_values: bfloat16 [2, 2048, 1024], P('dp', 'branch', 'tensor'), may hold values from -6 to 6
- keys: bfloat16 [2, 2048, 1024], P('dp', 'branch', 'tensor'), may hold values from -6 to 6
- values: bfloat16 [2, 2048, 1024], P('dp', 'branch', 'tensor'), may hold values from -6 to 6
- ancestors: int32 [2, 16, 2], P('dp'), may hold values from -1 to 15, as said below
- advantages: int32 [2, 2048], P('dp', 'branch'), may hold values from -4 to 4
- upstream: bfloat16 [2, 2048, 5120], P('dp', 'branch', 'tensor'), may hold values from -6 to 6
- out_weight: bfloat16 [5120, 8192], P(('dp', 'branch'), 'tensor'), may hold values from -0.0625 to 0.0625
Outputs:
- query_grad: bfloat16 [2, 2048, 8192], P('dp', 'branch', 'tensor')
- prefix_key_grad: bfloat16 [2, 2048, 1024], P('dp', 'branch', 'tensor')
- prefix_value_grad: bfloat16 [2, 2048, 1024], P('dp', 'branch', 'tensor')
- key_grad: bfloat16 [2, 2048, 1024], P('dp', 'branch', 'tensor')
- value_grad: bfloat16 [2, 2048, 1024], P('dp', 'branch', 'tensor')
- weight_grad: float32 [5120, 8192], P(('dp', 'branch'), 'tensor')
Inputs may be any that keep to these rules, and one draw needn't show every extreme that they name: ancestors[t, s, 0] is the parent and ancestors[t, s, 1] the grandparent of segment s in tree t, -1 where there is none; segments form up to three levels below the prefix, and every named segment is an ancestor on the path from s to the prefix.
All inputs are finite; a program needn't handle non-finite values.
Results may differ from a plain program's by a relative error of at most 0.03.
Values may be sent and summed in bfloat16 or wider, within the bound.
A program may use at most 128 MiB of HBM per device.

v0:
```python
import math

import jax
import jax.numpy as jnp
from jax import lax
from jax.sharding import PartitionSpec as P

H = 64
KVH = 8
HD = 128
SEG = 128


def block_grads(totals, blocks, key_head, value_head, allowed, score_scale):
    key_sum, value_sum = totals
    query_block, grad_block = blocks
    scores = (
        jnp.einsum("hqd,kd->hqk", query_block, key_head, preferred_element_type=jnp.float32)
        * score_scale
    )
    visible = allowed[None]
    row_max = jnp.max(jnp.where(visible, scores, -jnp.inf), axis=2, keepdims=True)
    exponent = jnp.where(visible, jnp.exp(scores - row_max), jnp.zeros_like(scores))
    shares = exponent / jnp.sum(exponent, axis=2, keepdims=True)
    shares_low = shares.astype(jnp.bfloat16)
    attn = jnp.einsum(
        "hqk,kd->hqd", shares_low, value_head, preferred_element_type=jnp.float32
    ).astype(jnp.bfloat16)
    grad_share = jnp.einsum(
        "hqd,kd->hqk", grad_block, value_head, preferred_element_type=jnp.float32
    )
    row_dot = jnp.sum(
        grad_block.astype(jnp.float32) * attn.astype(jnp.float32), axis=2, keepdims=True
    )
    grad_score = (shares * (grad_share - row_dot)).astype(jnp.bfloat16)
    grad_query = (
        jnp.einsum("hqk,kd->hqd", grad_score, key_head, preferred_element_type=jnp.float32)
        * score_scale
    ).astype(jnp.bfloat16)
    key_sum = key_sum + jnp.einsum(
        "hqk,hqd->kd", grad_score, query_block, preferred_element_type=jnp.float32
    )
    value_sum = value_sum + jnp.einsum(
        "hqk,hqd->kd", shares_low, grad_block, preferred_element_type=jnp.float32
    )
    return ((key_sum, value_sum), (grad_query, attn))


def on_device(
    queries, prefix_keys, prefix_values, keys, values, ancestors, advantages, upstream, out_weight
):
    local_queries = queries[0]
    tok_local = local_queries.shape[0]
    query_cols = local_queries.shape[1]
    kv_cols = keys.shape[2]
    group_size = H // KVH
    heads_here = query_cols // HD
    kv_here = kv_cols // HD
    score_scale = 1.0 / math.sqrt(HD)
    weighting = advantages[0].astype(jnp.float32) * 0.25
    cot_part = (upstream[0].astype(jnp.float32) * weighting[:, None]).astype(jnp.bfloat16)
    cotangent = lax.all_gather(cot_part, "tensor", axis=1, tiled=True)
    columns = cotangent
    d_attn = jnp.dot(
        columns,
        lax.all_gather(out_weight, ("dp", "branch"), axis=0, tiled=True),
        preferred_element_type=jnp.float32,
    ).astype(jnp.bfloat16)
    pre_keys, pre_values, seg_keys, seg_values = (
        lax.all_gather(prefix_keys[0], "branch", axis=0, tiled=True),
        lax.all_gather(prefix_values[0], "branch", axis=0, tiled=True),
        lax.all_gather(keys[0], "branch", axis=0, tiled=True),
        lax.all_gather(values[0], "branch", axis=0, tiled=True),
    )
    ctx_keys = jnp.concatenate([pre_keys, seg_keys], axis=0)
    ctx_values = jnp.concatenate([pre_values, seg_values], axis=0)
    prefix_len = pre_keys.shape[0]
    total_len = ctx_keys.shape[0]
    seg_here = tok_local // SEG
    first_seg = lax.axis_index("branch") * seg_here
    own_table = lax.dynamic_slice_in_dim(ancestors[0], first_seg, seg_here, 0)
    local_pos = jnp.arange(tok_local, dtype=jnp.int32)
    query_seg = first_seg + local_pos // SEG
    query_pos = local_pos % SEG
    lineage = jnp.repeat(own_table, SEG, axis=0)
    key_index = jnp.arange(total_len - prefix_len, dtype=jnp.int32)
    key_seg = key_index // SEG
    key_pos = key_index % SEG
    seg_seen = (key_seg[None, :] == lineage[:, 0:1]) | (key_seg[None, :] == lineage[:, 1:2])
    seg_seen = seg_seen | (key_seg[None, :] == query_seg[:, None]) & (
        key_pos[None, :] <= query_pos[:, None]
    )
    allowed = jnp.concatenate([jnp.ones((tok_local, prefix_len), dtype=bool), seg_seen], axis=1)
    per_block = math.gcd(group_size, max(1, 512 // tok_local))
    block_count = group_size // per_block
    query_heads = local_queries.reshape(tok_local, kv_here, block_count, per_block, HD).transpose(
        1, 2, 3, 0, 4
    )
    grad_heads = d_attn.reshape(tok_local, kv_here, block_count, per_block, HD).transpose(
        1, 2, 3, 0, 4
    )

    def advance(totals, blocks):
        return block_grads(totals, blocks, ctx_keys, ctx_values, allowed, score_scale)

    zeros_init = jnp.zeros((total_len, HD), jnp.float32)
    (key_sum, value_sum), (grad_query, attn) = lax.scan(
        advance, (zeros_init, zeros_init), (query_heads[0], grad_heads[0])
    )
    query_parts = [grad_query.reshape(group_size, tok_local, HD)]
    attn_parts = [attn.reshape(group_size, tok_local, HD)]
    key_parts = [key_sum]
    value_parts = [value_sum]
    query_grad = (
        jnp.stack(query_parts)
        .reshape(heads_here, tok_local, HD)
        .transpose(1, 0, 2)
        .reshape(tok_local, query_cols)
    )
    attn_flat = (
        jnp.stack(attn_parts)
        .reshape(heads_here, tok_local, HD)
        .transpose(1, 0, 2)
        .reshape(tok_local, query_cols)
    )
    key_total = jnp.stack(key_parts).transpose(1, 0, 2).reshape(total_len, kv_cols) * score_scale
    value_total = jnp.stack(value_parts).transpose(1, 0, 2).reshape(total_len, kv_cols)
    pre_key_grad, pre_value_grad, seg_key_grad, seg_value_grad = (
        lax.psum_scatter(key_total[:prefix_len], "branch", scatter_dimension=0, tiled=True),
        lax.psum_scatter(value_total[:prefix_len], "branch", scatter_dimension=0, tiled=True),
        lax.psum_scatter(key_total[prefix_len:], "branch", scatter_dimension=0, tiled=True),
        lax.psum_scatter(value_total[prefix_len:], "branch", scatter_dimension=0, tiled=True),
    )
    columns = cotangent
    weight_grad = lax.psum_scatter(
        lax.dot_general(
            columns, attn_flat, (((0,), (0,)), ((), ())), preferred_element_type=jnp.float32
        ),
        ("dp", "branch"),
        scatter_dimension=0,
        tiled=True,
    )
    return (
        query_grad[None],
        pre_key_grad.astype(jnp.bfloat16)[None],
        pre_value_grad.astype(jnp.bfloat16)[None],
        seg_key_grad.astype(jnp.bfloat16)[None],
        seg_value_grad.astype(jnp.bfloat16)[None],
        weight_grad,
    )


def solution(mesh):
    return jax.shard_map(
        on_device,
        mesh=mesh,
        in_specs=(
            P("dp", "branch", "tensor"),
            P("dp", "branch", "tensor"),
            P("dp", "branch", "tensor"),
            P("dp", "branch", "tensor"),
            P("dp", "branch", "tensor"),
            P("dp", None, None),
            P("dp", "branch"),
            P("dp", "branch", "tensor"),
            P(("dp", "branch"), "tensor"),
        ),
        out_specs=(
            P("dp", "branch", "tensor"),
            P("dp", "branch", "tensor"),
            P("dp", "branch", "tensor"),
            P("dp", "branch", "tensor"),
            P("dp", "branch", "tensor"),
            P(("dp", "branch"), "tensor"),
        ),
        check_vma=False,
    )
```

profile of v0, /device:TPU:0, one launch (start us, length us, event | category | flops | bytes accessed | tf_op | source)
XLA Modules:
  0.0 1039.2 jit_solution(18413001370826480079)
XLA Ops:
  8.0 1.8 fusion.33
  16.2 29.6 %all-gather.3 = bf16[1,2048,128]{1,2,0:T(8,128)(2,1)S(1)} all-gather(bf16[1,256,128]{1,2,0:T(8,128)(2,1)S(1)} %copy.33), channel_id=5, replica_groups=mesh['dp'=2,'branch'=8,'tensor'=8] {'branch'}, dimensions={1}, use_global_device_ids=true | all-gather | bytes 589824 | tf_op jit(solution)/shard_map/all_gather | solution.py:73
  45.8 36.8 %all-gather.2 = bf16[1,2048,128]{1,2,0:T(8,128)(2,1)S(1)} all-gather(bf16[1,256,128]{1,2,0:T(8,128)(2,1)S(1)} %copy.32), channel_id=4, replica_groups=mesh['dp'=2,'branch'=8,'tensor'=8] {'branch'}, dimensions={1}, use_global_device_ids=true | all-gather | bytes 589824 | tf_op jit(solution)/shard_map/all_gather | solution.py:71
  82.6 37.0 %all-gather = bf16[1,2048,128]{2,1,0:T(8,128)(2,1)S(1)} all-gather(bf16[1,256,128]{2,1,0:T(8,128)(2,1)S(1)} %copy-done.7), channel_id=2, replica_groups=mesh['dp'=2,'branch'=8,'tensor'=8] {'branch'}, dimensions={1}, use_global_device_ids=true | all-gather | bytes 589824 | tf_op jit(solution)/shard_map/all_gather | solution.py:70
  119.6 32.2 %all-gather.1 = bf16[1,2048,128]{2,1,0:T(8,128)(2,1)S(1)} all-gather(bf16[1,256,128]{2,1,0:T(8,128)(2,1)S(1)} %copy-done.8), channel_id=3, replica_groups=mesh['dp'=2,'branch'=8,'tensor'=8] {'branch'}, dimensions={1}, use_global_device_ids=true | all-gather | bytes 589824 | tf_op jit(solution)/shard_map/all_gather | solution.py:72
  154.0 133.8 %all-gather.9.cloned.1.call-done = bf16[5120,1024]{1,0:T(8,128)(2,1)} async-done(((bf16[320,1024]{1,0:T(8,128)(2,1)}), bf16[5120,1024]{1,0:T(8,128)(2,1)}) %all-gather.9.cloned.1.call-update) | async-done | bytes 10485776 | tf_op jit(solution)/shard_map/all_gather | solution.py:66
  287.8 8.5 convolution_convert_fusion.1
  296.3 2.2 reshape.83
  298.5 1.9 copy.51
  300.5 131.4 %while.17 = (s32[]{:T(128)}, f32[4096,128]{1,0:T(8,128)}, f32[4096,128]{1,0:T(8,128)S(1)}, bf16[4,2,256,128]{3,2,1,0:T(8,128)(2,1)}, bf16[4,2,256,128]{2,3,1,0:T...) while((s32[]{:T(128)}, f32[4096,128]{1,0:T(8,128)}, ...), condition=%wide.region_4.5_spmd.clone, body=%wide.region_0.4_spmd.clone.sunk | while | flops 3248950784 | bytes 105261304 | solution.py:107
  300.5 5.7 fusion.85
  306.2 10.1 fusion.86
  319.0 2.0 fusion.89
  321.1 2.8 multiply_convert_fusion.2
  324.6 4.8 fusion.90
  329.4 2.7 fusion.88
  332.1 5.7 fusion.85
  337.8 10.1 fusion.86
  350.7 2.1 fusion.89
  352.7 2.8 multiply_convert_fusion.2
  356.3 4.8 fusion.90
  361.1 4.3 fusion.88
  365.3 5.7 fusion.85
  371.1 10.1 fusion.86
  383.9 2.1 fusion.89
  386.0 2.8 multiply_convert_fusion.2
  389.5 4.8 fusion.90
  394.3 4.3 fusion.88
  398.6 5.7 fusion.85
  404.3 10.1 fusion.86
  415.8 1.3 multiply_reduce_fusion.2
  417.1 2.1 fusion.89
  419.2 2.8 multiply_convert_fusion.2
  422.8 4.8 fusion.90
  427.6 4.3 fusion.88
  431.8 1.8 broadcast_multiply_fusion
  433.6 1.4 fusion.46
  435.7 1.5 fusion.45
  437.9 10.5 %fusion.48 = f32[5120,1024]{1,0:T(8,128)} fusion(bf16[256,5120]{1,0:T(8,128)(2,1)} %all-gather.7.cloned.1.call-done, bf16[256,1024]{0,1:T(8,128)(2,1)S(1)} %bitcast.135), kind=kOutput, calls=%fused_computation.81 | convolution fusion | flops 2684354560 | bytes 24117248 | tf_op jit(solution)/shard_map/dot_general | solution.py:136
  450.8 26.8 %reduce-scatter.10.cloned.1.call-done = f32[256,128]{1,0:T(8,128)} async-done(((f32[2048,128]{1,0:T(8,128)}), f32[256,128]{1,0:T(8,128)}) %reduce-scatter.10.cloned.1.call-update) | async-done | bytes 131088 | tf_op jit(solution)/shard_map/reduce_scatter | solution.py:131
  477.6 1.5 convert_bitcast_fusion.1
  479.1 39.1 %reduce-scatter.6.cloned.1.call-done = f32[256,128]{1,0:T(8,128)} async-done(((f32[2048,128]{1,0:T(8,128)}), f32[256,128]{1,0:T(8,128)}) %reduce-scatter.6.cloned.1.call-update) | async-done | bytes 131088 | tf_op jit(solution)/shard_map/reduce_scatter | solution.py:129
  518.3 1.5 convert_bitcast_fusion.3
  519.8 38.9 %reduce-scatter.12.cloned.1.call-done = f32[256,128]{1,0:T(8,128)} async-done(((f32[2048,128]{1,0:T(8,128)}), f32[256,128]{1,0:T(8,128)}) %reduce-scatter.12.cloned.1.call-update) | async-done | bytes 131088 | tf_op jit(solution)/shard_map/reduce_scatter | solution.py:132
  558.7 1.5 convert_bitcast_fusion
  560.2 39.1 %reduce-scatter.8.cloned.1.call-done = f32[256,128]{1,0:T(8,128)} async-done(((f32[2048,128]{1,0:T(8,128)}), f32[256,128]{1,0:T(8,128)}) %reduce-scatter.8.cloned.1.call-update) | async-done | bytes 131088 | tf_op jit(solution)/shard_map/reduce_scatter | solution.py:130
  599.3 1.5 convert_bitcast_fusion.2
  600.8 431.5 %reduce-scatter.14.cloned.1.call-done = f32[320,1024]{1,0:T(8,128)} async-done(((f32[5120,1024]{1,0:T(8,128)}), f32[320,1024]{1,0:T(8,128)}) %reduce-scatter.14.cloned.1.call-update) | async-done | bytes 1310736 | tf_op jit(solution)/shard_map/reduce_scatter | solution.py:135
  (86 shorter events, 25.5 us)
Async XLA Ops:
  7.2 3.5 copy-start
  7.2 75.4 %copy-start.7 = (bf16[1,256,128]{2,1,0:T(8,128)(2,1)S(1)}, bf16[1,256,128]{2,1,0:T(8,128)(2,1)}, u32[]{:S(2)}) copy-start(bf16[1,256,128]{2,1,0:T(8,128)(2,1)} %param.12) | copy-start | bytes 196612
  7.2 112.4 %copy-start.8 = (bf16[1,256,128]{2,1,0:T(8,128)(2,1)S(1)}, bf16[1,256,128]{2,1,0:T(8,128)(2,1)}, u32[]{:S(2)}) copy-start(bf16[1,256,128]{2,1,0:T(8,128)(2,1)} %param.14) | copy-start | bytes 196612
  7.2 146.8 %all-gather.7.cloned.1.call-start = ((), (), s32[]{:S(2)}) async-start(), calls=%async_computation.5 | async-start | bytes 2949120 | tf_op jit(solution)/shard_map/all_gather | solution.py:62
  9.8 278.0 %all-gather.9.cloned.1.call-start = ((), (), s32[]{:S(2)}) async-start(), calls=%async_computation.6 | async-start | bytes 11141120 | tf_op jit(solution)/shard_map/all_gather | solution.py:66
  10.6 467.0 %reduce-scatter.10.cloned.1.call-start = ((), (), s32[]{:S(2)}) async-start(), calls=%async_computation.9 | async-start | bytes 1179648 | tf_op jit(solution)/shard_map/reduce_scatter | solution.py:131
  316.3 1.3 copy-start.3
  316.3 1.4 copy-start.4
  324.0 5.5 copy-start.2
  347.9 1.3 copy-start.3
  347.9 1.4 copy-start.4
  355.6 5.5 copy-start.2
  381.2 1.3 copy-start.3
  381.2 1.4 copy-start.4
  388.9 5.5 copy-start.2
  414.4 1.3 copy-start.3
  414.4 1.4 copy-start.4
  422.1 5.5 copy-start.2
  435.0 2.8 copy-start.5
  435.1 83.2 %reduce-scatter.6.cloned.1.call-start = ((), (), s32[]{:S(2)}) async-start(), calls=%async_computation.7 | async-start | bytes 1179648 | tf_op jit(solution)/shard_map/reduce_scatter | solution.py:129
  435.6 123.1 %reduce-scatter.12.cloned.1.call-start = ((), (), s32[]{:S(2)}) async-start(), calls=%async_computation.10 | async-start | bytes 1179648 | tf_op jit(solution)/shard_map/reduce_scatter | solution.py:132
  437.3 162.1 %reduce-scatter.8.cloned.1.call-start = ((), (), s32[]{:S(2)}) async-start(), calls=%async_computation.8 | async-start | bytes 1179648 | tf_op jit(solution)/shard_map/reduce_scatter | solution.py:130
  437.8 594.5 %reduce-scatter.14.cloned.1.call-start = ((), (), s32[]{:S(2)}) async-start(), calls=%async_computation.11 | async-start | bytes 22282240 | tf_op jit(solution)/shard_map/reduce_scatter | solution.py:135
  448.4 1.0 copy-start.6
  448.4 583.9 %copy-start.1 = (s32[1,16,2]{1,2,0:T(2,128)S(1)}, s32[1,16,2]{1,2,0:T(2,128)}, u32[]{:S(2)}) copy-start(s32[1,16,2]{1,2,0:T(2,128)} %param.16) | copy-start | bytes 388
Sparse Core Ops, SparseCore 0:
  10.0 28.8 all-gather.6
  40.4 247.3 all-gather.8
  435.2 42.3 reduce-scatter.9
  479.8 38.4 reduce-scatter.5
  520.5 38.1 reduce-scatter.11
  560.9 38.3 reduce-scatter.7
  602.3 429.9 reduce-scatter.13
where the time goes:
time: 1040 us
  waiting for transfers between devices  711 us (68%)
  blocking collectives  136 us (13%)
  matrix products  101 us (10%)
  other arithmetic  58.9 us (6%)
  local copies, waits for them, and re-layouts  17.7 us (2%)
  between operations  14.3 us (1%)
    reduce_scatter x1, waiting for transfers between devices, on_device(): lax.psum_scatter(lax.dot_general(columns, attn_flat, (((0,), (0,)), ((),...  431 us
    all_gather x1, waiting for transfers between devices, on_device(): lax.all_gather(out_weight, ('dp', 'branch'), axis=0, tiled=True)  134 us
    sub x4, other arithmetic, block_grads(): scores - row_max  40.3 us
    reduce_scatter x1, waiting for transfers between devices, on_device(): lax.psum_scatter(key_total[:prefix_len], 'branch', scatter_dimension=0, t...  39.1 us
    reduce_scatter x1, waiting for transfers between devices, on_device(): lax.psum_scatter(value_total[:prefix_len], 'branch', scatter_dimension=0,...  39.1 us
    reduce_scatter x1, waiting for transfers between devices, on_device(): lax.psum_scatter(value_total[prefix_len:], 'branch', scatter_dimension=0,...  38.9 us
    all_gather x1, blocking collectives, on_device(): lax.all_gather(prefix_keys[0], 'branch', axis=0, tiled=True)  37 us
    all_gather x1, blocking collectives, on_device(): lax.all_gather(prefix_values[0], 'branch', axis=0, tiled=True)  36.8 us
  transfers between devices with their start and end apart: 7, of which 6 were waited for; matrix products, arithmetic and copies ran while one was open for 3% of the time, Pallas kernels for 0%

commit v1 on v0

v1 whole, which is shorter than its diff:
```python
import math

import jax
import jax.numpy as jnp
from jax import lax
from jax.experimental import pallas as pl
from jax.experimental.pallas import tpu as pltpu
from jax.sharding import PartitionSpec as P

HD = 128
SEG = 128
GROUP = 8
TOKL = 256
KVB = 8
WROWS = 320
NCOL = 1024
UCOL = 640
CTX = 2048
SEGCTX = 384
ALLCTX = CTX + SEGCTX
ROWS = 512
SCALE = 1.0 / math.sqrt(HD)
LOG2E = 1.4426950408889634
BF = jnp.bfloat16
F32 = jnp.float32
VM = pl.BlockSpec(memory_space=pltpu.VMEM)
VLIM = 56 * 2**20


def coords():
    b = lax.axis_index("branch")
    t = lax.axis_index("tensor")
    return t // 2, b // 2, lax.axis_index("dp") * 2 + b % 2, t % 2


def place(x, y, z, c):
    return {"dp": z // 2, "branch": y * 2 + z % 2, "tensor": x * 2 + c}


def rcopy(src, dst, ss, rs, dev):
    return pltpu.make_async_remote_copy(
        src_ref=src, dst_ref=dst, send_sem=ss, recv_sem=rs,
        device_id=dev, device_id_type=pl.DeviceIdType.MESH,
    )


def signal(sem, dev):
    pl.semaphore_signal(sem, inc=1, device_id=dev, device_id_type=pl.DeviceIdType.MESH)


def nt_dot(a, b):
    return lax.dot_general(a, b, (((1,), (1,)), ((), ())), preferred_element_type=F32)


def gather_kernel(
    up, adv, w, pk, pv, sk, sv,
    dattn, kvg, cott,
    cot, cotb, wg, dpart, drecv,
    cot_s, cot_r, sib_s, sib_r, w_s, w_r, kz_s, kz_r, ko_s, ko_r, kf_s, kf_r, d_s, d_r,
):
    x, y, z, c = coords()
    me_b = y * 2 + z % 2
    sib_b = y * 2 + 1 - z % 2
    zsib = z + 1 - 2 * (z % 2)
    target_y = 2 * (x % 2) + c
    is_recv = c == y % 2
    self_send = target_y == y
    half = x // 2
    sib = place(x, y, z, 1 - c)

    bar = pltpu.get_barrier_semaphore()
    for d in range(1, 4):
        signal(bar, place(x, y, (z + d) % 4, c))
        signal(bar, place(x, (y + d) % 4, z, c))
    signal(bar, sib)

    @pl.when(is_recv)
    def _():
        for h in range(2):
            for yy in range(4):
                sx = 2 * h + y // 2

                @pl.when(jnp.logical_not((sx == x) & (yy == y)))
                def _():
                    signal(bar, place(sx, yy, z, c))

    kvg[0, me_b] = pk[...]
    kvg[1, me_b] = pv[...]
    kvg[2, me_b] = sk[...]
    kvg[3, me_b] = sv[...]
    wrow = jnp.broadcast_to(adv[...].astype(F32) * 0.25, (TOKL, TOKL))
    ri = lax.broadcasted_iota(jnp.int32, (TOKL, TOKL), 0)
    ci = lax.broadcasted_iota(jnp.int32, (TOKL, TOKL), 1)
    diag = jnp.where(ri == ci, wrow, 0.0).astype(BF)
    cot[...] = jnp.dot(diag, up[...], preferred_element_type=F32).astype(BF)

    pl.semaphore_wait(bar, 11 - self_send.astype(jnp.int32))

    def kz():
        return rcopy(kvg.at[:, me_b], kvg.at[:, me_b], kz_s, kz_r, place(x, y, zsib, c))

    def ko(d):
        return rcopy(kvg.at[:, me_b], kvg.at[:, me_b], ko_s.at[d - 1], ko_r.at[d - 1],
                     place(x, (y + d) % 4, z, c))

    def kf(d):
        return rcopy(kvg.at[:, sib_b], kvg.at[:, sib_b], kf_s.at[d - 1], kf_r.at[d - 1],
                     place(x, (y + d) % 4, z, c))

    def wc(d):
        return rcopy(w, wg.at[pl.ds(pl.multiple_of(z * WROWS, 64), WROWS)], w_s.at[d - 1], w_r.at[d - 1],
                     place(x, y, (z + d) % 4, c))

    def cc(d):
        return rcopy(cot, cotb.at[half, y], cot_s.at[d], cot_r.at[half, y],
                     place((x + d) % 4, target_y, z, c))

    kz().start()
    for d in (1, 3, 2):
        cc(d).start()

    @pl.when(jnp.logical_not(self_send))
    def _():
        cc(0).start()

    for d in (1, 3, 2):
        wc(d).start()
    for d in (1, 3, 2):
        ko(d).start()
    wg[pl.ds(pl.multiple_of(z * WROWS, 64), WROWS), :] = w[...]

    @pl.when(self_send)
    def _():
        cotb[half, y] = cot[...]

    kz().wait()
    for d in (1, 3, 2):
        kf(d).start()

    def sc(h, yy):
        return rcopy(cotb.at[h, yy], cotb.at[h, yy], sib_s.at[h, yy], sib_r.at[h, yy], sib)

    @pl.when(is_recv)
    def _():
        for h in range(2):
            for yy in range(4):
                @pl.when(jnp.logical_not((2 * h + y // 2 == x) & (yy == y)))
                def _():
                    rcopy(cot, cotb.at[h, yy], cot_s.at[0], cot_r.at[h, yy], sib).wait_recv()
                sc(h, yy).start()

    @pl.when(jnp.logical_not(is_recv))
    def _():
        for h in range(2):
            for yy in range(4):
                sc(h, yy).wait_recv()

    for d in range(1, 4):
        wc(d).wait()

    def block(yy):
        return jnp.dot(cotb[0, yy], wg[0:UCOL, :], preferred_element_type=F32) + jnp.dot(
            cotb[1, yy], wg[UCOL:2 * UCOL, :], preferred_element_type=F32)

    def dc(d):
        return rcopy(dpart.at[d - 1], drecv.at[d - 1], d_s.at[d - 1], d_r.at[d - 1],
                     place(x, (y + d) % 4, z, c))

    @pl.loop(1, 4)
    def _(d):
        dpart[d - 1] = block((y + d) % 4).astype(BF)
        dc(d).start()

    own = block(y)
    for h in range(2):
        for yy in range(4):
            cott[pl.ds(h * UCOL, UCOL), pl.ds(yy * TOKL, TOKL)] = cotb[h, yy].T

    for d in range(1, 4):
        dc(d).wait()
    dattn[...] = (own + drecv[0].astype(F32) + drecv[1].astype(F32) + drecv[2].astype(F32)).astype(BF)

    for d in range(1, 4):
        ko(d).wait()
        kf(d).wait()
        cc(d).wait_send()

    @pl.when(jnp.logical_not(self_send))
    def _():
        cc(0).wait_send()

    @pl.when(is_recv)
    def _():
        for h in range(2):
            for yy in range(4):
                sc(h, yy).wait_send()


def attention_kernel(anc, q, do, kv, dq, attn, dkv, s_f, p_b, kc, vc, dkt, dvt, segk, segv):
    first = lax.axis_index("branch") * 2
    cexp = SCALE * LOG2E
    chunks = [(i * 512, 512) for i in range(4)] + [(CTX, SEGCTX)]
    dkt[...] = jnp.zeros_like(dkt)
    dvt[...] = jnp.zeros_like(dvt)
    segk[...] = jnp.zeros_like(segk)
    segv[...] = jnp.zeros_like(segv)
    kc[0:CTX, :] = kv[0]
    vc[0:CTX, :] = kv[1]

    @pl.loop(0, 2)
    def _(s):
        seg = first + s
        a0 = anc[0, seg, 0]
        a1 = anc[0, seg, 1]
        for i, a in enumerate((a0, a1, seg)):
            rows = pl.ds(pl.multiple_of(jnp.maximum(a, 0) * SEG, SEG), SEG)
            kc[CTX + i * SEG:CTX + (i + 1) * SEG, :] = kv[2, rows, :]
            vc[CTX + i * SEG:CTX + (i + 1) * SEG, :] = kv[3, rows, :]
        dkt[:, CTX:] = jnp.zeros((HD, SEGCTX), F32)
        dvt[:, CTX:] = jnp.zeros((HD, SEGCTX), F32)
        tok = pl.ds(pl.multiple_of(s * SEG, SEG), SEG)
        col = lax.broadcasted_iota(jnp.int32, (ROWS, SEGCTX), 1)
        row = lax.broadcasted_iota(jnp.int32, (ROWS, SEGCTX), 0) % SEG
        seen = jnp.where(col < SEG, (a0 >= 0).astype(jnp.int32),
                         jnp.where(col < 2 * SEG, (a1 >= 0).astype(jnp.int32),
                                   (col - 2 * SEG <= row).astype(jnp.int32))) > 0

        for hb in range(GROUP * SEG // ROWS):
            nh = ROWS // SEG
            heads = [pl.ds((hb * nh + i) * HD, HD) for i in range(nh)]
            qb = jnp.concatenate([q[tok, h] for h in heads], axis=0)
            mx = None
            for st, n in chunks:
                sc = nt_dot(qb, kc[st:st + n, :])
                if st == CTX:
                    sc = jnp.where(seen, sc, -1e30)
                s_f[:, st:st + n] = sc
                for t in range(n // 128):
                    part = sc[:, t * 128:(t + 1) * 128]
                    mx = part if mx is None else jnp.maximum(mx, part)
            m = jnp.max(mx, axis=1, keepdims=True)
            lsum = None
            o = None
            for st, n in chunks:
                p = jnp.exp2((s_f[:, st:st + n] - m) * cexp)
                for t in range(n // 128):
                    part = p[:, t * 128:(t + 1) * 128]
                    lsum = part if lsum is None else lsum + part
                pb = p.astype(BF)
                p_b[:, st:st + n] = pb
                oc = jnp.dot(pb, vc[st:st + n, :], preferred_element_type=F32)
                o = oc if o is None else o + oc
            il = 1.0 / jnp.sum(lsum, axis=1, keepdims=True)
            ob = (o * il).astype(BF)
            for i, h in enumerate(heads):
                attn[tok, h] = ob[i * SEG:(i + 1) * SEG]
            dob = jnp.concatenate([do[tok, h] for h in heads], axis=0)
            dos = (dob.astype(F32) * il).astype(BF)
            delta = jnp.sum(dos.astype(F32) * ob.astype(F32), axis=1, keepdims=True)
            qt = qb.T
            dot_ = dos.T
            dqa = None
            for st, n in chunks:
                dp = nt_dot(dos, vc[st:st + n, :])
                pb = p_b[:, st:st + n]
                ds = (pb.astype(F32) * (dp - delta)).astype(BF)
                dqc = jnp.dot(ds, kc[st:st + n, :], preferred_element_type=F32)
                dqa = dqc if dqa is None else dqa + dqc
                dkt[:, st:st + n] += jnp.dot(qt, ds, preferred_element_type=F32)
                dvt[:, st:st + n] += jnp.dot(dot_, pb, preferred_element_type=F32)
            dqb = (dqa * SCALE).astype(BF)
            for i, h in enumerate(heads):
                dq[tok, h] = dqb[i * SEG:(i + 1) * SEG]

        for i, a in enumerate((a0, a1, seg)):
            cols = pl.ds(pl.multiple_of(jnp.maximum(a, 0) * SEG, SEG), SEG)
            segk[cols, :] += dkt[:, CTX + i * SEG:CTX + (i + 1) * SEG].T
            segv[cols, :] += dvt[:, CTX + i * SEG:CTX + (i + 1) * SEG].T

    for i in range(4):
        dkv[0, i * 512:(i + 1) * 512, :] = (dkt[:, i * 512:(i + 1) * 512].T * SCALE).astype(BF)
        dkv[1, i * 512:(i + 1) * 512, :] = dvt[:, i * 512:(i + 1) * 512].T.astype(BF)
    dkv[2] = (segk[...] * SCALE).astype(BF)
    dkv[3] = segv[...].astype(BF)


def reduce_kernel(
    attn, cott, dkv,
    opk, opv, osk, osv, owg,
    attng, gpart, grecv, krecv, kpart, zrecv,
    a_s, a_r, k_s, k_r, z_s, z_r, g_s, g_r,
):
    x, y, z, c = coords()
    zsib = z + 1 - 2 * (z % 2)
    bar = pltpu.get_barrier_semaphore()
    for d in range(1, 4):
        signal(bar, place(x, y, (z + d) % 4, c))
        signal(bar, place(x, (y + d) % 4, z, c))
    pl.semaphore_wait(bar, 6)

    def ac(d):
        return rcopy(attn, attng.at[pl.ds(pl.multiple_of(y * TOKL, TOKL), TOKL)], a_s.at[d - 1], a_r.at[d - 1],
                     place(x, (y + d) % 4, z, c))

    def kc(d):
        yy = (y + d) % 4
        return rcopy(dkv.at[:, pl.ds(pl.multiple_of(yy * 512, 512), 512)], krecv.at[d - 1], k_s.at[d - 1],
                     k_r.at[d - 1], place(x, yy, z, c))

    def gc(d):
        return rcopy(gpart.at[d - 1], grecv.at[d - 1], g_s.at[d - 1], g_r.at[d - 1],
                     place(x, y, (z + d) % 4, c))

    def zc():
        return rcopy(kpart, zrecv, z_s, z_r, place(x, y, zsib, c))

    for d in (1, 3, 2):
        ac(d).start()
    for d in (1, 3, 2):
        kc(d).start()
    attng[pl.ds(pl.multiple_of(y * TOKL, TOKL), TOKL), :] = attn[...]
    for d in range(1, 4):
        ac(d).wait()

    def block(zz):
        return jnp.dot(cott[pl.ds(pl.multiple_of(zz * WROWS, 64), WROWS), :], attng[...],
                       preferred_element_type=F32)

    @pl.loop(1, 4)
    def _(d):
        gpart[d - 1] = block((z + d) % 4).astype(BF)
        gc(d).start()

    owg[...] = block(z)
    for d in range(1, 4):
        kc(d).wait()
    zl = z % 2

    def ksum(i, zz):
        r = pl.ds(pl.multiple_of(zz * 256, 256), 256)
        own = dkv[i, pl.ds(pl.multiple_of(y * 512 + zz * 256, 256), 256), :].astype(F32)
        return own + krecv[0, i, r, :].astype(F32) + krecv[1, i, r, :].astype(F32) + krecv[2, i, r, :].astype(F32)

    for i in range(4):
        kpart[i] = ksum(i, 1 - zl).astype(BF)
    zc().start()
    zc().wait()
    for i, o in enumerate((opk, opv, osk, osv)):
        o[...] = (ksum(i, zl) + zrecv[i].astype(F32)).astype(BF)
    for d in range(1, 4):
        gc(d).wait()
    owg[...] += grecv[0].astype(F32) + grecv[1].astype(F32) + grecv[2].astype(F32)


def on_device(
    queries, prefix_keys, prefix_values, keys, values, ancestors, advantages, upstream, out_weight
):
    dma = pltpu.SemaphoreType.DMA
    sds = jax.ShapeDtypeStruct
    dattn, kvg, cott = pl.pallas_call(
        gather_kernel,
        out_shape=(
            sds((TOKL, NCOL), BF),
            sds((4, KVB, 256, HD), BF),
            sds((2 * UCOL, 4 * TOKL), BF),
        ),
        in_specs=[VM] * 7,
        out_specs=(VM, VM, VM),
        scratch_shapes=[
            pltpu.VMEM((TOKL, UCOL), BF),
            pltpu.VMEM((2, 4, TOKL, UCOL), BF),
            pltpu.VMEM((4 * WROWS, NCOL), BF),
            pltpu.VMEM((3, TOKL, NCOL), BF),
            pltpu.VMEM((3, TOKL, NCOL), BF),
            dma((4,)), dma((2, 4)), dma((2, 4)), dma((2, 4)),
            dma((3,)), dma((3,)), dma, dma, dma((3,)), dma((3,)), dma((3,)), dma((3,)),
            dma((3,)), dma((3,)),
        ],
        compiler_params=pltpu.CompilerParams(
            collective_id=0, has_side_effects=True, vmem_limit_bytes=VLIM),
        name="gather",
    )(upstream[0], advantages, out_weight, prefix_keys[0], prefix_values[0], keys[0], values[0])

    dq, attn, dkv = pl.pallas_call(
        attention_kernel,
        out_shape=(
            sds((TOKL, NCOL), BF),
            sds((TOKL, NCOL), BF),
            sds((4, CTX, HD), BF),
        ),
        in_specs=[pl.BlockSpec(memory_space=pltpu.SMEM), VM, VM, VM],
        out_specs=(VM, VM, VM),
        scratch_shapes=[
            pltpu.VMEM((ROWS, ALLCTX), F32),
            pltpu.VMEM((ROWS, ALLCTX), BF),
            pltpu.VMEM((ALLCTX, HD), BF),
            pltpu.VMEM((ALLCTX, HD), BF),
            pltpu.VMEM((HD, ALLCTX), F32),
            pltpu.VMEM((HD, ALLCTX), F32),
            pltpu.VMEM((CTX, HD), F32),
            pltpu.VMEM((CTX, HD), F32),
        ],
        compiler_params=pltpu.CompilerParams(vmem_limit_bytes=VLIM),
        name="attention",
    )(ancestors, queries[0], dattn, kvg.reshape(4, CTX, HD))

    opk, opv, osk, osv, owg = pl.pallas_call(
        reduce_kernel,
        out_shape=tuple([sds((256, HD), BF)] * 4 + [sds((WROWS, NCOL), F32)]),
        in_specs=[VM] * 3,
        out_specs=tuple([VM] * 5),
        scratch_shapes=[
            pltpu.VMEM((4 * TOKL, NCOL), BF),
            pltpu.VMEM((3, WROWS, NCOL), BF),
            pltpu.VMEM((3, WROWS, NCOL), BF),
            pltpu.VMEM((3, 4, 512, HD), BF),
            pltpu.VMEM((4, 256, HD), BF),
            pltpu.VMEM((4, 256, HD), BF),
            dma((3,)), dma((3,)), dma((3,)), dma((3,)), dma, dma, dma((3,)), dma((3,)),
        ],
        compiler_params=pltpu.CompilerParams(
            collective_id=1, has_side_effects=True, vmem_limit_bytes=VLIM),
        name="reduce",
    )(attn, cott, dkv)
    return dq[None], opk[None], opv[None], osk[None], osv[None], owg


def solution(mesh):
    return jax.shard_map(
        on_device,
        mesh=mesh,
        in_specs=(
            P("dp", "branch", "tensor"),
            P("dp", "branch", "tensor"),
            P("dp", "branch", "tensor"),
            P("dp", "branch", "tensor"),
            P("dp", "branch", "tensor"),
            P("dp", None, None),
            P("dp", "branch"),
            P("dp", "branch", "tensor"),
            P(("dp", "branch"), "tensor"),
        ),
        out_specs=(
            P("dp", "branch", "tensor"),
            P("dp", "branch", "tensor"),
            P("dp", "branch", "tensor"),
            P("dp", "branch", "tensor"),
            P("dp", "branch", "tensor"),
            P(("dp", "branch"), "tensor"),
        ),
        check_vma=False,
    )
```

time: 1040 us -> 177 us (0.17)
  waiting for transfers between devices: 711 us -> 0 us
  Pallas kernels: 0 us -> 166 us
  blocking collectives: 136 us -> 0 us
  matrix products: 101 us -> 0 us
  other arithmetic: 58.9 us -> 0 us
  between operations: 14.3 us -> 0.65 us
    reduce_scatter x5 -> x0, waiting for transfers between devices: 575 us -> none  [the longest x1 431 us: on_device(): lax.psum_scatter(lax.dot_general(columns, attn_flat, (((0,), (0,)), ((),...]
    pallas_call x0 -> x3, Pallas kernels: none -> 166 us  [the longest x1 73.4 us: on_device(): pl.pallas_call(gather_kernel, out_shape=(sds((TOKL, NCOL), BF), sds((4, K...]
    all_gather x4 -> x0, blocking collectives: 136 us -> none  [the longest x1 37 us: on_device(): lax.all_gather(prefix_keys[0], 'branch', axis=0, tiled=True)]
    all_gather x2 -> x0, waiting for transfers between devices: 134 us -> none  [the longest x1 134 us: on_device(): lax.all_gather(out_weight, ('dp', 'branch'), axis=0, tiled=True)]
    dot_general x26 -> x0, matrix products: 101 us -> none  [the longest x4 22.9 us: block_grads(): jnp.einsum('hqd,kd->hqk', query_block, key_head, preferred_element_type=j...]
    sub x4 -> x0, other arithmetic: 40.3 us -> none  [block_grads(): scores - row_max]
  transfers between devices with their start and end apart: 7 -> 0, of which waited for: 6 -> 0; matrix products, arithmetic and copies ran while one was open for 3% -> 0% of each run, Pallas kernels for 0% -> 0%
where the time goes in v1:
time: 177 us; the launch traced here: 176 us
  Pallas kernels  166 us (94%)
  local copies, waits for them, and re-layouts  9.77 us (6%)
    pallas_call x1, Pallas kernels, on_device(): pl.pallas_call(gather_kernel, out_shape=(sds((TOKL, NCOL), BF), sds((4, K...  73.4 us
    pallas_call x1, Pallas kernels, on_device(): pl.pallas_call(reduce_kernel, out_shape=tuple([sds((256, HD), BF)] * 4 +...  68.2 us
    pallas_call x1, Pallas kernels, on_device(): pl.pallas_call(attention_kernel, out_shape=(sds((TOKL, NCOL), BF), sds((T...  24.4 us
    unnamed x6, local copies, waits for them, and re-layouts  9.77 us

profile of v1, /device:TPU:0, one launch (start us, length us, event | category | flops | bytes accessed | tf_op | source)
XLA Modules:
  0.0 176.5 jit_solution(15470079874152651205)
XLA Ops:
  0.6 1.4 copy.15.anc
  2.0 73.4 %gather.1 = (bf16[256,1024]{1,0:T(8,128)(2,1)}, bf16[4,8,256,128]{3,2,1,0:T(8,128)(2,1)}, bf16[1280,1024]{1,0:T(8,128)(2,1)}) custom-call(bf16[256,640]{1,0:T(8,128)(2,1)} %bitcast.14, s32[1,256]{1,0:T(1,128)} %adv.1, bf16[320,1024]{1,0:T(8,128)(2,1)} %w.1, bf16[256,128]{1,0:T(8,128)(2,1)} %bitcast.15, bf16[256,128]{1,0:T(8,128)(2,1)} %bitcast.16, ...), custom_call_target="tpu_custom_call" | custom-call | tf_op jit(solution)/shard_map/gather/pallas_call | solution.py:360
  75.4 24.4 %attention.1 = (bf16[256,1024]{1,0:T(8,128)(2,1)}, bf16[256,1024]{1,0:T(8,128)(2,1)}, bf16[4,2048,128]{2,1,0:T(8,128)(2,1)}) custom-call(s32[1,16,2]{2,1,0:T(8,128)} %copy.15.anc, bf16[256,1024]{1,0:T(8,128)(2,1)} %bitcast.13, bf16[256,1024]{1,0:T(8,128)(2,1)} %get-tuple-element.17.do, bf16[4,2048,128]{2,1,0:T(8,128)(2,1)} %bitcast.12), custom_call_target="tpu_custom_call" | custom-call | tf_op jit(solution)/shard_map/attention/pallas_call | solution.py:384
  99.8 68.2 %reduce.1 = (bf16[256,128]{1,0:T(8,128)(2,1)}, bf16[256,128]{1,0:T(8,128)(2,1)}, bf16[256,128]{1,0:T(8,128)(2,1)}, bf16[256,128]{1,0:T(8,128)(2,1)}, f32[320,1024]{1,0:T(8,128)}) custom-call(bf16[256,1024]{1,0:T(8,128)(2,1)} %get-tuple-element.20.attn, bf16[1280,1024]{1,0:T(8,128)(2,1)} %get-tuple-element.21.cott, bf16[4,2048,128]{2,1,0:T(8,128)(2,1)} %get-tuple-element.22.dkv), custom_call_target="tpu_custom_call" | custom-call | tf_op jit(solution)/shard_map/reduce/pallas_call | solution.py:407
  168.1 1.5 copy.21
  169.6 1.5 copy.22
  171.0 1.5 copy.23
  172.5 1.5 copy.24
  174.0 2.5 %copy.25 = f32[320,1024]{1,0:T(8,128)} copy(f32[320,1024]{1,0:T(8,128)} %get-tuple-element.39) | data formatting | bytes 2621440

commit v2 on v0

v2 whole, which is shorter than its diff:
```python
import math

import jax
import jax.numpy as jnp
from jax import lax
from jax.experimental import pallas as pl
from jax.experimental.pallas import tpu as pltpu
from jax.sharding import PartitionSpec as P

HD = 128
SEG = 128
GROUP = 8
TOKL = 256
KVB = 8
WROWS = 320
NCOL = 1024
UCOL = 640
CTX = 2048
SEGCTX = 384
ALLCTX = CTX + SEGCTX
CH = 512
ROWS = 512
SCALE = 1.0 / math.sqrt(HD)
LOG2E = 1.4426950408889634
BF = jnp.bfloat16
F32 = jnp.float32
VM = pl.BlockSpec(memory_space=pltpu.VMEM)
VLIM = 60 * 2**20


def coords():
    b = lax.axis_index("branch")
    t = lax.axis_index("tensor")
    return t // 2, b // 2, lax.axis_index("dp") * 2 + b % 2, t % 2


def place(x, y, z, c):
    return {"dp": z // 2, "branch": y * 2 + z % 2, "tensor": x * 2 + c}


def rcopy(src, dst, ss, rs, dev):
    return pltpu.make_async_remote_copy(
        src_ref=src, dst_ref=dst, send_sem=ss, recv_sem=rs,
        device_id=dev, device_id_type=pl.DeviceIdType.MESH,
    )


def signal(sem, dev):
    pl.semaphore_signal(sem, inc=1, device_id=dev, device_id_type=pl.DeviceIdType.MESH)


def nt_dot(a, b):
    return lax.dot_general(a, b, (((1,), (1,)), ((), ())), preferred_element_type=F32)


class GatherRing:
    def __init__(self, me, dev, view, ss, rs):
        self.me, self.dev, self.view, self.ss, self.rs = me, dev, view, ss, rs

    def copy(self, node, piece, kind, step):
        v = self.view(node, piece)
        i = kind * 2 + piece
        return rcopy(v, v, self.ss.at[i], self.rs.at[i], self.dev(step))

    def right(self, p):
        return self.copy(self.me, p, 0, 1)

    def left(self, p):
        return self.copy(self.me, p, 1, 3)

    def fwd(self, p):
        if p == 0:
            return self.copy((self.me + 3) % 4, 0, 2, 1)
        return self.copy((self.me + 1) % 4, 1, 2, 3)

    def send(self, p):
        self.right(p).start()
        self.left(p).start()

    def forward(self, p):
        (self.right if p == 0 else self.left)(p).wait_recv()
        self.fwd(p).start()

    def wait_near(self):
        self.right(1).wait_recv()
        self.left(0).wait_recv()

    def wait_far(self):
        self.fwd(0).wait_recv()
        self.fwd(1).wait_recv()

    def wait_sends(self):
        for p in range(2):
            self.right(p).wait_send()
            self.left(p).wait_send()
            self.fwd(p).wait_send()


class SumRing:
    def __init__(self, dev, sb, rb, ss, rs):
        self.dev, self.sb, self.rb, self.ss, self.rs = dev, sb, rb, ss, rs

    def copy(self, i):
        return rcopy(self.sb.at[i], self.rb.at[i], self.ss.at[i], self.rs.at[i], self.dev(1 if i % 2 == 0 else 3))

    def send(self, i, value):
        self.sb[i] = value.astype(BF)
        self.copy(i).start()

    def add_send(self, i, value):
        self.copy(i - 4).wait_recv()
        self.send(i, value + self.rb[i - 4].astype(F32))

    def wait_result(self):
        for i in range(2, 6):
            self.copy(i).wait_recv()

    def result(self, p, own):
        a, b = ((4, 3), (2, 5))[p]
        return own + self.rb[a].astype(F32) + self.rb[b].astype(F32)

    def wait_sends(self):
        for i in range(6):
            self.copy(i).wait_send()


def whole_kernel(
    anc, up, adv, w, pk, pv, sk, sv, q,
    odq, okv, owg,
    cot, cotb, cott, wg, kvg, kcs, vcs,
    dsb, drb, dnear, dattn,
    s_f, p_b, p_s, attng, il_b, delta, qt, dos, dost, dqa,
    acc, accs, segt, ksb, krb, zsb, zrb, kown,
    gsb, grb, gnear,
    c_s, c_r, x_s, x_r, b_s, b_r, w_s, w_r, kz_s, kz_r, k_s, k_r,
    d_s, d_r, a_s, a_r, r_s, r_r, zk_s, zk_r, g_s, g_r,
):
    x, y, z, c = coords()
    zl = z % 2
    first = lax.axis_index("branch") * 2
    target_y = 2 * (x % 2) + c
    is_recv = c == y % 2
    is_src = target_y == y
    half = x // 2
    sib = place(x, y, z, 1 - c)
    cexp = SCALE * LOG2E

    def ydev(d):
        return place(x, (y + d) % 4, z, c)

    def zdev(d):
        return place(x, y, (z + d) % 4, c)

    bar = pltpu.get_barrier_semaphore()
    for d in range(1, 4):
        signal(bar, ydev(d))
    signal(bar, zdev(1))
    signal(bar, zdev(3))
    signal(bar, sib)

    @pl.when(is_recv)
    def _():
        for h in range(2):
            sx = 2 * h + y // 2

            @pl.when(sx != x)
            def _():
                signal(bar, place(sx, y, z, c))

    rows_b = lambda b: pl.ds(pl.multiple_of(b * 256, 256), 256)
    own_rows = rows_b(y * 2 + zl)
    for i, r in enumerate((pk, pv, sk, sv)):
        kvg[i, own_rows, :] = r[...]
    wrow = jnp.broadcast_to(adv[...].astype(F32) * 0.25, (TOKL, TOKL))
    ri = lax.broadcasted_iota(jnp.int32, (TOKL, TOKL), 0)
    ci = lax.broadcasted_iota(jnp.int32, (TOKL, TOKL), 1)
    diag = jnp.where(ri == ci, wrow, 0.0).astype(BF)
    cot[...] = jnp.dot(diag, up[...], preferred_element_type=F32).astype(BF)
    w_half = WROWS // 2
    wview = lambda n, p: wg.at[pl.ds(pl.multiple_of(n * WROWS + p * w_half, 32), w_half)]
    wg[pl.ds(pl.multiple_of(z * WROWS, 64), WROWS), :] = w[...]

    pl.semaphore_wait(bar, 6 + 3 * is_src.astype(jnp.int32))

    wring = GatherRing(z, zdev, wview, w_s, w_r)
    kring = GatherRing(y, ydev, lambda n, p: kvg.at[:, rows_b(n * 2 + p)], k_s, k_r)
    aring = GatherRing(
        y, ydev, lambda n, p: attng.at[pl.ds(pl.multiple_of(n * TOKL + p * SEG, SEG), SEG)], a_s, a_r)
    dring = SumRing(ydev, dsb, drb, d_s, d_r)
    rring = SumRing(ydev, ksb, krb, r_s, r_r)
    gring = SumRing(zdev, gsb, grb, g_s, g_r)

    def kz():
        v = kvg.at[:, own_rows]
        return rcopy(v, v, kz_s, kz_r, place(x, y, z + 1 - 2 * zl, c))

    def cy():
        return rcopy(cot, cotb.at[half, y], c_s, c_r.at[y], place(x, target_y, z, c))

    def cx(yy, d):
        v = cotb.at[half, yy]
        return rcopy(v, v, x_s.at[yy, d - 1], x_r.at[half, yy], place((x + d) % 4, y, z, c))

    def cb(h, yy):
        v = cotb.at[h, yy]
        return rcopy(v, v, b_s.at[h, yy], b_r.at[h, yy], sib)

    kz().start()

    @pl.when(jnp.logical_not(is_src))
    def _():
        cy().start()

    kring.send(zl)
    for p in range(2):
        wring.send(p)

    @pl.when(is_src)
    def _():
        cotb[half, y] = cot[...]
        for k in range(4):
            yy = (y + (0, 1, 3, 2)[k]) % 4
            if k > 0:
                rcopy(cot, cotb.at[half, yy], c_s, c_r.at[yy], sib).wait_recv()
            for d in (1, 3, 2):
                cx(yy, d).start()
            cb(half, yy).start()

    kz().wait_recv()
    kring.send(1 - zl)

    @pl.when(is_recv)
    def _():
        for yy in range(4):
            for h in range(2):
                @pl.when(jnp.logical_not(is_src & (half == h)))
                def _():
                    v = cotb.at[h, yy]
                    rcopy(v, v, b_s.at[h, yy], x_r.at[h, yy], sib).wait_recv()
                    cb(h, yy).start()

    for p in range(2):
        kring.forward(p)
    for p in range(2):
        wring.forward(p)
    kring.wait_near()
    kring.wait_far()

    named = [[jnp.broadcast_to(anc[0, pl.ds(first + s, 1), i:i + 1], (1, HD)) for i in range(2)] for s in range(2)]

    def hot(s, i, j):
        return (named[s][i] == j).astype(F32)

    for s in range(2):
        own_seg = pl.ds(pl.multiple_of((first + s) * SEG, SEG), SEG)
        for k, dst in enumerate((kcs, vcs)):
            for i in range(2):
                tot = None
                for j in range(16):
                    v = kvg[2 + k, j * SEG:(j + 1) * SEG, :].astype(F32) * hot(s, i, j)
                    tot = v if tot is None else tot + v
                dst[s, i * SEG:(i + 1) * SEG, :] = tot.astype(BF)
            dst[s, 2 * SEG:, :] = kvg[2 + k, own_seg, :]

    nh = ROWS // SEG

    def forward(rb):
        s, hb = rb // 2, rb % 2
        tok = slice(s * SEG, (s + 1) * SEG)
        rows = slice(rb * ROWS, (rb + 1) * ROWS)
        col = lax.broadcasted_iota(jnp.int32, (ROWS, SEG), 1)
        row = lax.broadcasted_iota(jnp.int32, (ROWS, SEG), 0) % SEG
        shut = [jnp.where(named[s][i] >= 0, 0.0, -1e30) for i in range(2)]
        shut.append(jnp.where(col <= row, 0.0, -1e30))
        heads = [slice((hb * nh + i) * HD, (hb * nh + i + 1) * HD) for i in range(nh)]
        qb = jnp.concatenate([q[tok, h] for h in heads], axis=0)
        qt[rb] = qb.T
        mx = None
        for j in range(5):
            kc = kvg[0, j * CH:(j + 1) * CH, :] if j < 4 else kcs[s]
            sc = nt_dot(qb, kc)
            n = sc.shape[1]
            if j == 4:
                sc = jnp.concatenate([sc[:, i * SEG:(i + 1) * SEG] + shut[i] for i in range(3)], axis=1)
            s_f[:, j * CH:j * CH + n] = sc
            for t in range(n // 128):
                part = sc[:, t * 128:(t + 1) * 128]
                mx = part if mx is None else jnp.maximum(mx, part)
        m = jnp.max(mx, axis=1, keepdims=True)
        lsum = None
        o = None
        for j in range(5):
            vc = kvg[1, j * CH:(j + 1) * CH, :] if j < 4 else vcs[s]
            n = vc.shape[0]
            p = jnp.exp2((s_f[:, j * CH:j * CH + n] - m) * cexp)
            for t in range(n // 128):
                part = p[:, t * 128:(t + 1) * 128]
                lsum = part if lsum is None else lsum + part
            pb = p.astype(BF)
            if j < 4:
                p_b[j, rows, :] = pb
            else:
                p_s[rows, :] = pb
            oc = jnp.dot(pb, vc, preferred_element_type=F32)
            o = oc if o is None else o + oc
        il = jnp.broadcast_to(1.0 / jnp.sum(lsum, axis=1, keepdims=True), (ROWS, HD))
        il_b[rows, :] = il
        ob = (o * il).astype(BF)
        for i, h in enumerate(heads):
            attng[pl.ds(pl.multiple_of(y * TOKL + s * SEG, SEG), SEG), h] = ob[i * SEG:(i + 1) * SEG]

    forward(0)

    wring.wait_near()
    wring.wait_far()

    @pl.when(jnp.logical_not(is_recv))
    def _():
        for h in range(2):
            for yy in range(4):
                cb(h, yy).wait_recv()

    def proj(yy, rows):
        return jnp.dot(cotb[0, yy, rows, :], wg[0:UCOL, :], preferred_element_type=F32) + jnp.dot(
            cotb[1, yy, rows, :], wg[UCOL:2 * UCOL, :], preferred_element_type=F32)

    lo, hi = slice(0, SEG), slice(SEG, 2 * SEG)
    dring.send(0, proj((y + 2) % 4, lo))
    dring.send(1, proj((y + 2) % 4, hi))
    dring.send(2, proj((y + 1) % 4, hi))
    dring.send(3, proj((y + 3) % 4, lo))
    dnear[0] = proj((y + 1) % 4, lo)
    dnear[1] = proj((y + 3) % 4, hi)
    dnear[2] = proj(y, lo)
    dnear[3] = proj(y, hi)

    forward(1)
    dring.add_send(4, dnear[0])
    dring.add_send(5, dnear[1])
    aring.send(0)
    forward(2)
    forward(3)
    aring.send(1)
    for h in range(2):
        for yy in range(4):
            cott[h * UCOL:(h + 1) * UCOL, yy * TOKL:(yy + 1) * TOKL] = cotb[h, yy].T

    dring.wait_result()
    for p in range(2):
        dattn[p * SEG:(p + 1) * SEG, :] = dring.result(p, dnear[2 + p]).astype(BF)
    for rb in range(4):
        s, hb = rb // 2, rb % 2
        rows = slice(rb * ROWS, (rb + 1) * ROWS)
        tok = slice(s * SEG, (s + 1) * SEG)
        arow = pl.ds(pl.multiple_of(y * TOKL + s * SEG, SEG), SEG)
        heads = [slice((hb * nh + i) * HD, (hb * nh + i + 1) * HD) for i in range(nh)]
        dob = jnp.concatenate([dattn[tok, h] for h in heads], axis=0)
        at = jnp.concatenate([attng[arow, h] for h in heads], axis=0)
        db = (dob.astype(F32) * il_b[rows, :]).astype(BF)
        dos[rows, :] = db
        dost[rb] = db.T
        dl = jnp.sum(db.astype(F32) * at.astype(F32), axis=1, keepdims=True)
        delta[rows, :] = jnp.broadcast_to(dl, (ROWS, HD))

    aring.forward(0)

    def back(rb, kc, vc, pb):
        rows = pl.ds(pl.multiple_of(rb * ROWS, ROWS), ROWS)
        dl = delta[rows, :]
        n = vc.shape[0]
        dp = nt_dot(dos[rows, :], vc)
        ds = (pb.astype(F32) * (dp - jnp.concatenate([dl] * (n // HD), axis=1))).astype(BF)
        return (rows, jnp.dot(ds, kc, preferred_element_type=F32),
                jnp.dot(qt[rb], ds, preferred_element_type=F32),
                jnp.dot(dost[rb], pb, preferred_element_type=F32))

    for rb in range(4):
        s = rb // 2
        rows, dqc, dk, dv = back(rb, kcs[s], vcs[s], p_s[rb * ROWS:(rb + 1) * ROWS, :])
        dqa[rows, :] = dqc
        if rb % 2 == 0:
            accs[s, 0] = dk
            accs[s, 1] = dv
        else:
            accs[s, 0] += dk
            accs[s, 1] += dv
    for j in range(16):
        for k in range(2):
            tot = None
            for s in range(2):
                for i in range(2):
                    v = accs[s, k, :, i * SEG:(i + 1) * SEG] * hot(s, i, j)
                    tot = v if tot is None else tot + v
            segt[j // 4, k, :, (j % 4) * SEG:(j % 4 + 1) * SEG] = tot
    for s in range(2):
        own_cols = pl.ds(pl.multiple_of((zl * 2 + s) * SEG, SEG), SEG)
        for k in range(2):
            segt[y, k, :, own_cols] += accs[s, k, :, 2 * SEG:]
    rring.send(0, segt[(y + 2) % 4])
    rring.send(3, segt[(y + 3) % 4])

    def prefix(j):
        acc[...] = jnp.zeros_like(acc)
        crow = pl.ds(pl.multiple_of(j * CH, CH), CH)

        @pl.loop(0, 4)
        def _(rb):
            rows = pl.ds(pl.multiple_of(rb * ROWS, ROWS), ROWS)
            _, dqc, dk, dv = back(rb, kvg[0, crow, :], kvg[1, crow, :], p_b[j, rows, :])
            dqa[rows, :] += dqc
            acc[0] += dk
            acc[1] += dv

    prefix((y + 2) % 4)
    rring.send(1, acc[...])
    aring.forward(1)
    prefix((y + 1) % 4)
    rring.send(2, acc[...])
    rring.add_send(4, segt[(y + 1) % 4])
    prefix((y + 3) % 4)
    rring.add_send(5, acc[...])

    aring.wait_near()
    aring.wait_far()

    def wgrad(zz, p):
        rows = pl.ds(pl.multiple_of(zz * WROWS + p * w_half, 32), w_half)
        return jnp.dot(cott[rows, :], attng[...], preferred_element_type=F32)

    gring.send(0, wgrad((z + 2) % 4, 0))
    gring.send(1, wgrad((z + 2) % 4, 1))
    gring.send(2, wgrad((z + 1) % 4, 1))
    gring.send(3, wgrad((z + 3) % 4, 0))
    gnear[0] = wgrad((z + 1) % 4, 0)
    gnear[1] = wgrad((z + 3) % 4, 1)

    prefix(y)
    for rb in range(4):
        s, hb = rb // 2, rb % 2
        dqb = (dqa[rb * ROWS:(rb + 1) * ROWS, :] * SCALE).astype(BF)
        for i in range(nh):
            odq[s * SEG:(s + 1) * SEG, (hb * nh + i) * HD:(hb * nh + i + 1) * HD] = dqb[i * SEG:(i + 1) * SEG]

    gring.add_send(4, gnear[0])
    gring.add_send(5, gnear[1])
    for p in range(2):
        owg[p * w_half:(p + 1) * w_half, :] = wgrad(z, p)

    rring.wait_result()
    kown[0:2] = rring.result(1, acc[...])
    kown[2:4] = rring.result(0, segt[y])
    lanes = lambda v: pl.ds(pl.multiple_of(v * 256, 256), 256)
    zsb[...] = kown[:, :, lanes(1 - zl)].astype(BF)

    def zk():
        return rcopy(zsb, zrb, zk_s, zk_r, place(x, y, z + 1 - 2 * zl, c))

    zk().start()
    zk().wait_recv()
    for i in range(4):
        t = kown[i, :, lanes(zl)] + zrb[i].astype(F32)
        if i % 2 == 0:
            t = t * SCALE
        okv[i] = t.T.astype(BF)

    gring.wait_result()
    for p in range(2):
        rows = slice(p * w_half, (p + 1) * w_half)
        owg[rows, :] = gring.result(p, owg[rows, :])

    kz().wait_send()
    zk().wait_send()

    @pl.when(jnp.logical_not(is_src))
    def _():
        cy().wait_send()

    @pl.when(is_src)
    def _():
        for yy in range(4):
            for d in range(1, 4):
                cx(yy, d).wait_send()

    @pl.when(is_recv)
    def _():
        for h in range(2):
            for yy in range(4):
                cb(h, yy).wait_send()

    for ring in (wring, kring, aring, dring, rring, gring):
        ring.wait_sends()


def finish_kernel(dq, kv, wgr, o0, o1, o2, o3, o4, o5):
    o0[...] = dq[...]
    for i, o in enumerate((o1, o2, o3, o4)):
        o[...] = kv[i]
    o5[...] = wgr[...]


def on_device(
    queries, prefix_keys, prefix_values, keys, values, ancestors, advantages, upstream, out_weight
):
    dma = pltpu.SemaphoreType.DMA
    sds = jax.ShapeDtypeStruct
    vm = pltpu.VMEM
    half_w = WROWS // 2
    dq, okv, owg = pl.pallas_call(
        whole_kernel,
        out_shape=(
            sds((TOKL, NCOL), BF),
            sds((4, 256, HD), BF),
            sds((WROWS, NCOL), F32),
        ),
        in_specs=[VM] * 9,
        out_specs=(VM, VM, VM),
        scratch_shapes=[
            vm((TOKL, UCOL), BF),
            vm((2, 4, TOKL, UCOL), BF),
            vm((2 * UCOL, 4 * TOKL), BF),
            vm((4 * WROWS, NCOL), BF),
            vm((4, CTX, HD), BF),
            vm((2, SEGCTX, HD), BF),
            vm((2, SEGCTX, HD), BF),
            vm((6, SEG, NCOL), BF),
            vm((6, SEG, NCOL), BF),
            vm((4, SEG, NCOL), F32),
            vm((TOKL, NCOL), BF),
            vm((ROWS, ALLCTX), F32),
            vm((4, 4 * ROWS, CH), BF),
            vm((4 * ROWS, SEGCTX), BF),
            vm((4 * TOKL, NCOL), BF),
            vm((4 * ROWS, HD), F32),
            vm((4 * ROWS, HD), F32),
            vm((4, HD, ROWS), BF),
            vm((4 * ROWS, HD), BF),
            vm((4, HD, ROWS), BF),
            vm((4 * ROWS, HD), F32),
            vm((2, HD, CH), F32),
            vm((2, 2, HD, SEGCTX), F32),
            vm((4, 2, HD, CH), F32),
            vm((6, 2, HD, CH), BF),
            vm((6, 2, HD, CH), BF),
            vm((4, HD, 256), BF),
            vm((4, HD, 256), BF),
            vm((4, HD, CH), F32),
            vm((6, half_w, NCOL), BF),
            vm((6, half_w, NCOL), BF),
            vm((2, half_w, NCOL), F32),
            dma, dma((4,)), dma((4, 3)), dma((2, 4)), dma((2, 4)), dma((2, 4)),
            dma((6,)), dma((6,)), dma, dma, dma((6,)), dma((6,)),
            dma((6,)), dma((6,)), dma((6,)), dma((6,)), dma((6,)), dma((6,)),
            dma, dma, dma((6,)), dma((6,)),
        ],
        compiler_params=pltpu.CompilerParams(
            collective_id=0, has_side_effects=True, vmem_limit_bytes=VLIM),
        name="whole",
    )(ancestors, upstream[0], advantages, out_weight, prefix_keys[0], prefix_values[0], keys[0], values[0],
      queries[0])
    outs = pl.pallas_call(
        finish_kernel,
        out_shape=tuple([sds((TOKL, NCOL), BF)] + [sds((256, HD), BF)] * 4 + [sds((WROWS, NCOL), F32)]),
        in_specs=[VM] * 3,
        out_specs=tuple([VM] * 6),
        name="finish",
    )(dq, okv, owg)
    return tuple(o[None] for o in outs[:5]) + (outs[5],)


def solution(mesh):
    return jax.shard_map(
        on_device,
        mesh=mesh,
        in_specs=(
            P("dp", "branch", "tensor"),
            P("dp", "branch", "tensor"),
            P("dp", "branch", "tensor"),
            P("dp", "branch", "tensor"),
            P("dp", "branch", "tensor"),
            P("dp", None, None),
            P("dp", "branch"),
            P("dp", "branch", "tensor"),
            P(("dp", "branch"), "tensor"),
        ),
        out_specs=(
            P("dp", "branch", "tensor"),
            P("dp", "branch", "tensor"),
            P("dp", "branch", "tensor"),
            P("dp", "branch", "tensor"),
            P("dp", "branch", "tensor"),
            P(("dp", "branch"), "tensor"),
        ),
        check_vma=False,
    )
```

time: 1040 us -> 135 us (0.13)
  waiting for transfers between devices: 711 us -> 0 us
  blocking collectives: 136 us -> 0 us
  Pallas kernels: 0 us -> 132 us
  matrix products: 101 us -> 0 us
  other arithmetic: 58.9 us -> 0 us
  local copies, waits for them, and re-layouts: 17.7 us -> 1.35 us
  between operations: 14.3 us -> 0.64 us
    reduce_scatter x5 -> x0, waiting for transfers between devices: 575 us -> none  [the longest x1 431 us: on_device(): lax.psum_scatter(lax.dot_general(columns, attn_flat, (((0,), (0,)), ((),...]
    all_gather x4 -> x0, blocking collectives: 136 us -> none  [the longest x1 37 us: on_device(): lax.all_gather(prefix_keys[0], 'branch', axis=0, tiled=True)]
    all_gather x2 -> x0, waiting for transfers between devices: 134 us -> none  [the longest x1 134 us: on_device(): lax.all_gather(out_weight, ('dp', 'branch'), axis=0, tiled=True)]
    pallas_call x0 -> x2, Pallas kernels: none -> 132 us  [the longest x1 129 us: on_device(): pl.pallas_call(whole_kernel, out_shape=(sds((TOKL, NCOL), BF), sds((4, 25...]
    dot_general x26 -> x0, matrix products: 101 us -> none  [the longest x4 22.9 us: block_grads(): jnp.einsum('hqd,kd->hqk', query_block, key_head, preferred_element_type=j...]
    sub x4 -> x0, other arithmetic: 40.3 us -> none  [block_grads(): scores - row_max]
  transfers between devices with their start and end apart: 7 -> 0, of which waited for: 6 -> 0; matrix products, arithmetic and copies ran while one was open for 3% -> 0% of each run, Pallas kernels for 0% -> 0%
where the time goes in v2:
time: 135 us; the launch traced here: 134 us
  Pallas kernels  132 us (98%)
  local copies, waits for them, and re-layouts  1.35 us (1%)
    pallas_call x1, Pallas kernels, on_device(): pl.pallas_call(whole_kernel, out_shape=(sds((TOKL, NCOL), BF), sds((4, 25...  129 us
    pallas_call x1, Pallas kernels, on_device(): pl.pallas_call(finish_kernel, out_shape=tuple([sds((TOKL, NCOL), BF)] + [...  2.89 us

profile of v2, /device:TPU:0, one launch (start us, length us, event | category | flops | bytes accessed | tf_op | source)
XLA Modules:
  0.0 133.9 jit_solution(8920696163635736969)
XLA Ops:
  0.6 1.4 %copy.15.anc = s32[1,16,2]{2,1,0:T(8,128)} copy(s32[1,16,2]{1,2,0:T(2,128)} %param.14) | data formatting | bytes 256 | tf_op args[5]
  2.0 129.0 %whole.1 = (bf16[256,1024]{1,0:T(8,128)(2,1)}, bf16[4,256,128]{2,1,0:T(8,128)(2,1)}, f32[320,1024]{1,0:T(8,128)}) custom-call(s32[1,16,2]{2,1,0:T(8,128)} %copy.15.anc, bf16[256,640]{1,0:T(8,128)(2,1)} %bitcast.12, s32[1,256]{1,0:T(1,128)} %adv.1, bf16[320,1024]{1,0:T(8,128)(2,1)} %w.1, bf16[256,128]{1,0:T(8,128)(2,1)} %bitcast.13, ...), custom_call_target="tpu_custom_call" | custom-call | tf_op jit(solution)/shard_map/whole/pallas_call | solution.py:508
  131.0 2.9 %finish.1 = (bf16[256,1024]{1,0:T(8,128)(2,1)}, bf16[256,128]{1,0:T(8,128)(2,1)}, bf16[256,128]{1,0:T(8,128)(2,1)}, bf16[256,128]{1,0:T(8,128)(2,1)}, bf16[256,128]{1,0:T(8,128)(2,1)}, /*index=5*/f32[320,1024]{1,0:T(8,128)}) custom-call(bf16[256,1024]{1,0:T(8,128)(2,1)} %get-tuple-element.15.dq, bf16[4,256,128]{2,1,0:T(8,128)(2,1)} %get-tuple-element.16.kv, ...), custom_call_target="tpu_custom_call" | custom-call | tf_op jit(solution)/shard_map/finish/pallas_call | solution.py:560

commit v3 on v2

--- a/solution.py
+++ b/solution.py
@@ -151,6 +151,9 @@
     def zdev(d):
         return place(x, y, (z + d) % 4, c)
 
+    def xdev(d):
+        return place((x + d) % 4, y, z, c)
+
     bar = pltpu.get_barrier_semaphore()
     for d in range(1, 4):
         signal(bar, ydev(d))
@@ -160,12 +163,8 @@
 
     @pl.when(is_recv)
     def _():
-        for h in range(2):
-            sx = 2 * h + y // 2
-
-            @pl.when(sx != x)
-            def _():
-                signal(bar, place(sx, y, z, c))
+        signal(bar, xdev(1))
+        signal(bar, xdev(3))
 
     rows_b = lambda b: pl.ds(pl.multiple_of(b * 256, 256), 256)
     own_rows = rows_b(y * 2 + zl)
@@ -180,7 +179,7 @@
     wview = lambda n, p: wg.at[pl.ds(pl.multiple_of(n * WROWS + p * w_half, 32), w_half)]
     wg[pl.ds(pl.multiple_of(z * WROWS, 64), WROWS), :] = w[...]
 
-    pl.semaphore_wait(bar, 6 + 3 * is_src.astype(jnp.int32))
+    pl.semaphore_wait(bar, 6 + 2 * is_recv.astype(jnp.int32))
 
     wring = GatherRing(z, zdev, wview, w_s, w_r)
     kring = GatherRing(y, ydev, lambda n, p: kvg.at[:, rows_b(n * 2 + p)], k_s, k_r)
@@ -197,14 +196,35 @@
     def cy():
         return rcopy(cot, cotb.at[half, y], c_s, c_r.at[y], place(x, target_y, z, c))
 
-    def cx(yy, d):
-        v = cotb.at[half, yy]
-        return rcopy(v, v, x_s.at[yy, d - 1], x_r.at[half, yy], place((x + d) % 4, y, z, c))
+    def cx(h, yy, k):
+        v = cotb.at[h, yy]
+        return rcopy(v, v, x_s.at[yy, k], x_r.at[h, yy], xdev((1, 3)[k]))
 
     def cb(h, yy):
         v = cotb.at[h, yy]
         return rcopy(v, v, b_s.at[h, yy], b_r.at[h, yy], sib)
 
+    is_mid = is_recv & jnp.logical_not(is_src)
+    left_half = ((x + 3) % 4) // 2
+    right_half = ((x + 1) % 4) // 2
+
+    def mid_block(d):
+        yy = (y + d) % 4
+        cx(left_half, yy, 0).wait_recv()
+
+        @pl.when(yy < 2)
+        def _():
+            cx(left_half, yy, 0).start()
+
+        cb(left_half, yy).start()
+        cx(right_half, yy, 1).wait_recv()
+
+        @pl.when(yy >= 2)
+        def _():
+            cx(right_half, yy, 1).start()
+
+        cb(right_half, yy).start()
+
     kz().start()
 
     @pl.when(jnp.logical_not(is_src))
@@ -212,35 +232,59 @@
         cy().start()
 
     kring.send(zl)
-    for p in range(2):
-        wring.send(p)
+
+    @pl.when(zl == 0)
+    def _():
+        for p in range(2):
+            wring.left(p).start()
+
+    @pl.when(zl == 1)
+    def _():
+        for p in range(2):
+            wring.right(p).start()
 
     @pl.when(is_src)
     def _():
         cotb[half, y] = cot[...]
-        for k in range(4):
-            yy = (y + (0, 1, 3, 2)[k]) % 4
-            if k > 0:
-                rcopy(cot, cotb.at[half, yy], c_s, c_r.at[yy], sib).wait_recv()
-            for d in (1, 3, 2):
-                cx(yy, d).start()
-            cb(half, yy).start()
+        for k in range(2):
+            cx(half, y, k).start()
+        cb(half, y).start()
 
     kz().wait_recv()
     kring.send(1 - zl)
 
-    @pl.when(is_recv)
-    def _():
-        for yy in range(4):
-            for h in range(2):
-                @pl.when(jnp.logical_not(is_src & (half == h)))
-                def _():
-                    v = cotb.at[h, yy]
-                    rcopy(v, v, b_s.at[h, yy], x_r.at[h, yy], sib).wait_recv()
-                    cb(h, yy).start()
+    @pl.when(zl == 0)
+    def _():
+        for p in range(2):
+            wring.right(p).start()
+
+    @pl.when(zl == 1)
+    def _():
+        for p in range(2):
+            wring.left(p).start()
+
+    @pl.when(is_src)
+    def _():
+        for d in (1, 3, 2):
+            yy = (y + d) % 4
+            rcopy(cot, cotb.at[half, yy], c_s, c_r.at[yy], sib).wait_recv()
+            for k in range(2):
+                cx(half, yy, k).start()
+            cb(half, yy).start()
+
+    @pl.when(is_mid)
+    def _():
+        mid_block(0)
+        mid_block(1)
 
     for p in range(2):
         kring.forward(p)
+
+    @pl.when(is_mid)
+    def _():
+        mid_block(3)
+        mid_block(2)
+
     for p in range(2):
         wring.forward(p)
     kring.wait_near()
@@ -310,6 +354,18 @@
             attng[pl.ds(pl.multiple_of(y * TOKL + s * SEG, SEG), SEG), h] = ob[i * SEG:(i + 1) * SEG]
 
     forward(0)
+    forward(1)
+    aring.send(0)
+    forward(2)
+
+    @pl.when(is_src)
+    def _():
+        for d in (0, 1, 3, 2):
+            cx(1 - half, (y + d) % 4, 0).wait_recv()
+            cb(1 - half, (y + d) % 4).start()
+
+    forward(3)
+    aring.send(1)
 
     wring.wait_near()
     wring.wait_far()
@@ -334,16 +390,27 @@
     dnear[2] = proj(y, lo)
     dnear[3] = proj(y, hi)
 
-    forward(1)
-    dring.add_send(4, dnear[0])
-    dring.add_send(5, dnear[1])
-    aring.send(0)
-    forward(2)
-    forward(3)
-    aring.send(1)
     for h in range(2):
         for yy in range(4):
             cott[h * UCOL:(h + 1) * UCOL, yy * TOKL:(yy + 1) * TOKL] = cotb[h, yy].T
+    for p in range(2):
+        aring.forward(p)
+    dring.add_send(4, dnear[0])
+    dring.add_send(5, dnear[1])
+
+    aring.wait_near()
+    aring.wait_far()
+
+    def wgrad(zz, p):
+        rows = pl.ds(pl.multiple_of(zz * WROWS + p * w_half, 32), w_half)
+        return jnp.dot(cott[rows, :], attng[...], preferred_element_type=F32)
+
+    gring.send(0, wgrad((z + 2) % 4, 0))
+    gring.send(1, wgrad((z + 2) % 4, 1))
+    gring.send(2, wgrad((z + 1) % 4, 1))
+    gring.send(3, wgrad((z + 3) % 4, 0))
+    gnear[0] = wgrad((z + 1) % 4, 0)
+    gnear[1] = wgrad((z + 3) % 4, 1)
 
     dring.wait_result()
     for p in range(2):
@@ -361,8 +428,6 @@
         dost[rb] = db.T
         dl = jnp.sum(db.astype(F32) * at.astype(F32), axis=1, keepdims=True)
         delta[rows, :] = jnp.broadcast_to(dl, (ROWS, HD))
-
-    aring.forward(0)
 
     def back(rb, kc, vc, pb):
         rows = pl.ds(pl.multiple_of(rb * ROWS, ROWS), ROWS)
@@ -413,27 +478,13 @@
 
     prefix((y + 2) % 4)
     rring.send(1, acc[...])
-    aring.forward(1)
+    gring.add_send(4, gnear[0])
+    gring.add_send(5, gnear[1])
+    rring.add_send(4, segt[(y + 1) % 4])
     prefix((y + 1) % 4)
     rring.send(2, acc[...])
-    rring.add_send(4, segt[(y + 1) % 4])
     prefix((y + 3) % 4)
     rring.add_send(5, acc[...])
-
-    aring.wait_near()
-    aring.wait_far()
-
-    def wgrad(zz, p):
-        rows = pl.ds(pl.multiple_of(zz * WROWS + p * w_half, 32), w_half)
-        return jnp.dot(cott[rows, :], attng[...], preferred_element_type=F32)
-
-    gring.send(0, wgrad((z + 2) % 4, 0))
-    gring.send(1, wgrad((z + 2) % 4, 1))
-    gring.send(2, wgrad((z + 1) % 4, 1))
-    gring.send(3, wgrad((z + 3) % 4, 0))
-    gnear[0] = wgrad((z + 1) % 4, 0)
-    gnear[1] = wgrad((z + 3) % 4, 1)
-
     prefix(y)
     for rb in range(4):
         s, hb = rb // 2, rb % 2
@@ -441,35 +492,37 @@
         for i in range(nh):
             odq[s * SEG:(s + 1) * SEG, (hb * nh + i) * HD:(hb * nh + i + 1) * HD] = dqb[i * SEG:(i + 1) * SEG]
 
-    gring.add_send(4, gnear[0])
-    gring.add_send(5, gnear[1])
     for p in range(2):
         owg[p * w_half:(p + 1) * w_half, :] = wgrad(z, p)
 
-    rring.wait_result()
-    kown[0:2] = rring.result(1, acc[...])
-    kown[2:4] = rring.result(0, segt[y])
     lanes = lambda v: pl.ds(pl.multiple_of(v * 256, 256), 256)
-    zsb[...] = kown[:, :, lanes(1 - zl)].astype(BF)
-
-    def zk():
-        return rcopy(zsb, zrb, zk_s, zk_r, place(x, y, z + 1 - 2 * zl, c))
-
-    zk().start()
-    zk().wait_recv()
-    for i in range(4):
-        t = kown[i, :, lanes(zl)] + zrb[i].astype(F32)
-        if i % 2 == 0:
-            t = t * SCALE
-        okv[i] = t.T.astype(BF)
+
+    def zk(p):
+        return rcopy(zsb.at[p], zrb.at[p], zk_s.at[p], zk_r.at[p], place(x, y, z + 1 - 2 * zl, c))
+
+    for p in range(2):
+        for i in ((4, 3), (2, 5))[p]:
+            rring.copy(i).wait_recv()
+        kown[p] = rring.result(p, segt[y] if p == 0 else acc[...])
+        zsb[p] = kown[p, :, :, lanes(1 - zl)].astype(BF)
+        zk(p).start()
 
     gring.wait_result()
     for p in range(2):
         rows = slice(p * w_half, (p + 1) * w_half)
         owg[rows, :] = gring.result(p, owg[rows, :])
 
+    for p in range(2):
+        zk(p).wait_recv()
+        for i in range(2):
+            t = kown[p, i, :, lanes(zl)] + zrb[p, i].astype(F32)
+            if i == 0:
+                t = t * SCALE
+            okv[2 * (1 - p) + i] = t.T.astype(BF)
+
     kz().wait_send()
-    zk().wait_send()
+    for p in range(2):
+        zk(p).wait_send()
 
     @pl.when(jnp.logical_not(is_src))
     def _():
@@ -478,8 +531,13 @@
     @pl.when(is_src)
     def _():
         for yy in range(4):
-            for d in range(1, 4):
-                cx(yy, d).wait_send()
+            for k in range(2):
+                cx(half, yy, k).wait_send()
+
+    @pl.when(is_mid)
+    def _():
+        for yy in range(4):
+            cx(0, yy, yy // 2).wait_send()
 
     @pl.when(is_recv)
     def _():
@@ -541,16 +599,16 @@
             vm((4, 2, HD, CH), F32),
             vm((6, 2, HD, CH), BF),
             vm((6, 2, HD, CH), BF),
-            vm((4, HD, 256), BF),
-            vm((4, HD, 256), BF),
-            vm((4, HD, CH), F32),
+            vm((2, 2, HD, 256), BF),
+            vm((2, 2, HD, 256), BF),
+            vm((2, 2, HD, CH), F32),
             vm((6, half_w, NCOL), BF),
             vm((6, half_w, NCOL), BF),
             vm((2, half_w, NCOL), F32),
-            dma, dma((4,)), dma((4, 3)), dma((2, 4)), dma((2, 4)), dma((2, 4)),
+            dma, dma((4,)), dma((4, 2)), dma((2, 4)), dma((2, 4)), dma((2, 4)),
             dma((6,)), dma((6,)), dma, dma, dma((6,)), dma((6,)),
             dma((6,)), dma((6,)), dma((6,)), dma((6,)), dma((6,)), dma((6,)),
-            dma, dma, dma((6,)), dma((6,)),
+            dma((2,)), dma((2,)), dma((6,)), dma((6,)),
         ],
         compiler_params=pltpu.CompilerParams(
             collective_id=0, has_side_effects=True, vmem_limit_bytes=VLIM),

time: 135 us -> 107 us (0.79)
  Pallas kernels: 132 us -> 105 us
    pallas_call x1, Pallas kernels: 129 us -> 102 us  [on_device(): pl.pallas_call(whole_kernel, out_shape=(sds((TOKL, NCOL), BF), sds((4, 25...]
where the time goes in v3:
time: 107 us
  Pallas kernels  105 us (98%)
  local copies, waits for them, and re-layouts  1.35 us (1%)
    pallas_call x1, Pallas kernels, on_device(): pl.pallas_call(whole_kernel, out_shape=(sds((TOKL, NCOL), BF), sds((4, 25...  102 us
    pallas_call x1, Pallas kernels, on_device(): pl.pallas_call(finish_kernel, out_shape=tuple([sds((TOKL, NCOL), BF)] + [...  2.89 us

profile of v3, /device:TPU:0, one launch (start us, length us, event | category | flops | bytes accessed | tf_op | source)
XLA Modules:
  0.0 107.1 jit_solution(16410815605569143535)
XLA Ops:
  0.6 1.4 %copy.15.anc = s32[1,16,2]{2,1,0:T(8,128)} copy(s32[1,16,2]{1,2,0:T(2,128)} %param.14) | data formatting | bytes 256 | tf_op args[5]
  2.0 102.2 %whole.1 = (bf16[256,1024]{1,0:T(8,128)(2,1)}, bf16[4,256,128]{2,1,0:T(8,128)(2,1)}, f32[320,1024]{1,0:T(8,128)}) custom-call(s32[1,16,2]{2,1,0:T(8,128)} %copy.15.anc, bf16[256,640]{1,0:T(8,128)(2,1)} %bitcast.12, s32[1,256]{1,0:T(1,128)} %adv.1, bf16[320,1024]{1,0:T(8,128)(2,1)} %w.1, bf16[256,128]{1,0:T(8,128)(2,1)} %bitcast.13, ...), custom_call_target="tpu_custom_call" | custom-call | tf_op jit(solution)/shard_map/whole/pallas_call | solution.py:566
  104.2 2.9 %finish.1 = (bf16[256,1024]{1,0:T(8,128)(2,1)}, bf16[256,128]{1,0:T(8,128)(2,1)}, bf16[256,128]{1,0:T(8,128)(2,1)}, bf16[256,128]{1,0:T(8,128)(2,1)}, bf16[256,128]{1,0:T(8,128)(2,1)}, /*index=5*/f32[320,1024]{1,0:T(8,128)}) custom-call(bf16[256,1024]{1,0:T(8,128)(2,1)} %get-tuple-element.15.dq, bf16[4,256,128]{2,1,0:T(8,128)(2,1)} %get-tuple-element.16.kv, ...), custom_call_target="tpu_custom_call" | custom-call | tf_op jit(solution)/shard_map/finish/pallas_call | solution.py:618

commit v4 on v3

--- a/solution.py
+++ b/solution.py
@@ -357,15 +357,15 @@
     forward(1)
     aring.send(0)
     forward(2)
+    forward(3)
+    aring.send(1)
+    aring.forward(0)
 
     @pl.when(is_src)
     def _():
         for d in (0, 1, 3, 2):
             cx(1 - half, (y + d) % 4, 0).wait_recv()
             cb(1 - half, (y + d) % 4).start()
-
-    forward(3)
-    aring.send(1)
 
     wring.wait_near()
     wring.wait_far()
@@ -385,6 +385,7 @@
     dring.send(1, proj((y + 2) % 4, hi))
     dring.send(2, proj((y + 1) % 4, hi))
     dring.send(3, proj((y + 3) % 4, lo))
+    aring.forward(1)
     dnear[0] = proj((y + 1) % 4, lo)
     dnear[1] = proj((y + 3) % 4, hi)
     dnear[2] = proj(y, lo)
@@ -393,8 +394,6 @@
     for h in range(2):
         for yy in range(4):
             cott[h * UCOL:(h + 1) * UCOL, yy * TOKL:(yy + 1) * TOKL] = cotb[h, yy].T
-    for p in range(2):
-        aring.forward(p)
     dring.add_send(4, dnear[0])
     dring.add_send(5, dnear[1])
 
@@ -411,6 +410,8 @@
     gring.send(3, wgrad((z + 3) % 4, 0))
     gnear[0] = wgrad((z + 1) % 4, 0)
     gnear[1] = wgrad((z + 3) % 4, 1)
+    gring.add_send(4, gnear[0])
+    gring.add_send(5, gnear[1])
 
     dring.wait_result()
     for p in range(2):
@@ -478,8 +479,6 @@
 
     prefix((y + 2) % 4)
     rring.send(1, acc[...])
-    gring.add_send(4, gnear[0])
-    gring.add_send(5, gnear[1])
     rring.add_send(4, segt[(y + 1) % 4])
     prefix((y + 1) % 4)
     rring.send(2, acc[...])

time: 107 us -> 113 us (1.056)
  Pallas kernels: 105 us -> 111 us
    pallas_call x1, Pallas kernels: 102 us -> 108 us  [on_device(): pl.pallas_call(whole_kernel, out_shape=(sds((TOKL, NCOL), BF), sds((4, 25...]
where the time goes in v4:
time: 113 us
  Pallas kernels  111 us (98%)
  local copies, waits for them, and re-layouts  1.35 us (1%)
    pallas_call x1, Pallas kernels, on_device(): pl.pallas_call(whole_kernel, out_shape=(sds((TOKL, NCOL), BF), sds((4, 25...  108 us
    pallas_call x1, Pallas kernels, on_device(): pl.pallas_call(finish_kernel, out_shape=tuple([sds((TOKL, NCOL), BF)] + [...  2.89 us

profile of v4, /device:TPU:0, one launch (start us, length us, event | category | flops | bytes accessed | tf_op | source)
XLA Modules:
  0.0 112.7 jit_solution(15252245354944117472)
XLA Ops:
  0.6 1.4 %copy.15.anc = s32[1,16,2]{2,1,0:T(8,128)} copy(s32[1,16,2]{1,2,0:T(2,128)} %param.14) | data formatting | bytes 256 | tf_op args[5]
  2.0 107.8 %whole.1 = (bf16[256,1024]{1,0:T(8,128)(2,1)}, bf16[4,256,128]{2,1,0:T(8,128)(2,1)}, f32[320,1024]{1,0:T(8,128)}) custom-call(s32[1,16,2]{2,1,0:T(8,128)} %copy.15.anc, bf16[256,640]{1,0:T(8,128)(2,1)} %bitcast.12, s32[1,256]{1,0:T(1,128)} %adv.1, bf16[320,1024]{1,0:T(8,128)(2,1)} %w.1, bf16[256,128]{1,0:T(8,128)(2,1)} %bitcast.13, ...), custom_call_target="tpu_custom_call" | custom-call | tf_op jit(solution)/shard_map/whole/pallas_call | solution.py:565
  109.8 2.9 %finish.1 = (bf16[256,1024]{1,0:T(8,128)(2,1)}, bf16[256,128]{1,0:T(8,128)(2,1)}, bf16[256,128]{1,0:T(8,128)(2,1)}, bf16[256,128]{1,0:T(8,128)(2,1)}, bf16[256,128]{1,0:T(8,128)(2,1)}, /*index=5*/f32[320,1024]{1,0:T(8,128)}) custom-call(bf16[256,1024]{1,0:T(8,128)(2,1)} %get-tuple-element.15.dq, bf16[4,256,128]{2,1,0:T(8,128)(2,1)} %get-tuple-element.16.kv, ...), custom_call_target="tpu_custom_call" | custom-call | tf_op jit(solution)/shard_map/finish/pallas_call | solution.py:617

commit v5 on v4

--- a/solution.py
+++ b/solution.py
@@ -184,7 +184,7 @@
     wring = GatherRing(z, zdev, wview, w_s, w_r)
     kring = GatherRing(y, ydev, lambda n, p: kvg.at[:, rows_b(n * 2 + p)], k_s, k_r)
     aring = GatherRing(
-        y, ydev, lambda n, p: attng.at[pl.ds(pl.multiple_of(n * TOKL + p * SEG, SEG), SEG)], a_s, a_r)
+        y, ydev, lambda n, p: attng.at[p, pl.ds(pl.multiple_of(n * TOKL, TOKL), TOKL)], a_s, a_r)
     dring = SumRing(ydev, dsb, drb, d_s, d_r)
     rring = SumRing(ydev, ksb, krb, r_s, r_r)
     gring = SumRing(zdev, gsb, grb, g_s, g_r)
@@ -290,10 +290,12 @@
     kring.wait_near()
     kring.wait_far()
 
-    named = [[jnp.broadcast_to(anc[0, pl.ds(first + s, 1), i:i + 1], (1, HD)) for i in range(2)] for s in range(2)]
+    lane = lax.broadcasted_iota(jnp.int32, (1, 16), 1)
+    named = [[jnp.broadcast_to(jnp.sum(jnp.where(lane == first + s, anc[i:i + 1, :].astype(F32), 0.0),
+                                       axis=1, keepdims=True), (1, HD)) for i in range(2)] for s in range(2)]
 
     def hot(s, i, j):
-        return (named[s][i] == j).astype(F32)
+        return (named[s][i] == float(j)).astype(F32)
 
     for s in range(2):
         own_seg = pl.ds(pl.multiple_of((first + s) * SEG, SEG), SEG)
@@ -350,16 +352,13 @@
         il = jnp.broadcast_to(1.0 / jnp.sum(lsum, axis=1, keepdims=True), (ROWS, HD))
         il_b[rows, :] = il
         ob = (o * il).astype(BF)
-        for i, h in enumerate(heads):
-            attng[pl.ds(pl.multiple_of(y * TOKL + s * SEG, SEG), SEG), h] = ob[i * SEG:(i + 1) * SEG]
+        for i in range(nh):
+            attng[hb, pl.ds(pl.multiple_of(y * TOKL + s * SEG, SEG), SEG), i * HD:(i + 1) * HD] = (
+                ob[i * SEG:(i + 1) * SEG])
 
     forward(0)
-    forward(1)
+    forward(2)
     aring.send(0)
-    forward(2)
-    forward(3)
-    aring.send(1)
-    aring.forward(0)
 
     @pl.when(is_src)
     def _():
@@ -385,33 +384,30 @@
     dring.send(1, proj((y + 2) % 4, hi))
     dring.send(2, proj((y + 1) % 4, hi))
     dring.send(3, proj((y + 3) % 4, lo))
-    aring.forward(1)
     dnear[0] = proj((y + 1) % 4, lo)
     dnear[1] = proj((y + 3) % 4, hi)
     dnear[2] = proj(y, lo)
     dnear[3] = proj(y, hi)
 
+    forward(1)
+    aring.forward(0)
+    forward(3)
+    dring.add_send(4, dnear[0])
+    dring.add_send(5, dnear[1])
     for h in range(2):
         for yy in range(4):
             cott[h * UCOL:(h + 1) * UCOL, yy * TOKL:(yy + 1) * TOKL] = cotb[h, yy].T
-    dring.add_send(4, dnear[0])
-    dring.add_send(5, dnear[1])
-
-    aring.wait_near()
-    aring.wait_far()
 
     def wgrad(zz, p):
-        rows = pl.ds(pl.multiple_of(zz * WROWS + p * w_half, 32), w_half)
-        return jnp.dot(cott[rows, :], attng[...], preferred_element_type=F32)
-
+        rows = pl.ds(pl.multiple_of(zz * WROWS, 64), WROWS)
+        return jnp.dot(cott[rows, :], attng[p], preferred_element_type=F32)
+
+    aring.left(0).wait_recv()
+    aring.fwd(0).wait_recv()
     gring.send(0, wgrad((z + 2) % 4, 0))
-    gring.send(1, wgrad((z + 2) % 4, 1))
-    gring.send(2, wgrad((z + 1) % 4, 1))
     gring.send(3, wgrad((z + 3) % 4, 0))
     gnear[0] = wgrad((z + 1) % 4, 0)
-    gnear[1] = wgrad((z + 3) % 4, 1)
-    gring.add_send(4, gnear[0])
-    gring.add_send(5, gnear[1])
+    aring.send(1)
 
     dring.wait_result()
     for p in range(2):
@@ -423,7 +419,7 @@
         arow = pl.ds(pl.multiple_of(y * TOKL + s * SEG, SEG), SEG)
         heads = [slice((hb * nh + i) * HD, (hb * nh + i + 1) * HD) for i in range(nh)]
         dob = jnp.concatenate([dattn[tok, h] for h in heads], axis=0)
-        at = jnp.concatenate([attng[arow, h] for h in heads], axis=0)
+        at = jnp.concatenate([attng[hb, arow, i * HD:(i + 1) * HD] for i in range(nh)], axis=0)
         db = (dob.astype(F32) * il_b[rows, :]).astype(BF)
         dos[rows, :] = db
         dost[rb] = db.T
@@ -477,11 +473,20 @@
             acc[0] += dk
             acc[1] += dv
 
+    gring.add_send(4, gnear[0])
+    aring.forward(1)
     prefix((y + 2) % 4)
     rring.send(1, acc[...])
-    rring.add_send(4, segt[(y + 1) % 4])
     prefix((y + 1) % 4)
     rring.send(2, acc[...])
+    rring.add_send(4, segt[(y + 1) % 4])
+
+    aring.right(1).wait_recv()
+    aring.fwd(1).wait_recv()
+    gring.send(1, wgrad((z + 2) % 4, 1))
+    gring.send(2, wgrad((z + 1) % 4, 1))
+    gnear[1] = wgrad((z + 3) % 4, 1)
+
     prefix((y + 3) % 4)
     rring.add_send(5, acc[...])
     prefix(y)
@@ -491,8 +496,9 @@
         for i in range(nh):
             odq[s * SEG:(s + 1) * SEG, (hb * nh + i) * HD:(hb * nh + i + 1) * HD] = dqb[i * SEG:(i + 1) * SEG]
 
-    for p in range(2):
-        owg[p * w_half:(p + 1) * w_half, :] = wgrad(z, p)
+    gring.add_send(5, gnear[1])
+    for p in range(2):
+        owg[:, p * CH:(p + 1) * CH] = wgrad(z, p)
 
     lanes = lambda v: pl.ds(pl.multiple_of(v * 256, 256), 256)
 
@@ -508,8 +514,8 @@
 
     gring.wait_result()
     for p in range(2):
-        rows = slice(p * w_half, (p + 1) * w_half)
-        owg[rows, :] = gring.result(p, owg[rows, :])
+        cols = slice(p * CH, (p + 1) * CH)
+        owg[:, cols] = gring.result(p, owg[:, cols])
 
     for p in range(2):
         zk(p).wait_recv()
@@ -561,7 +567,6 @@
     dma = pltpu.SemaphoreType.DMA
     sds = jax.ShapeDtypeStruct
     vm = pltpu.VMEM
-    half_w = WROWS // 2
     dq, okv, owg = pl.pallas_call(
         whole_kernel,
         out_shape=(
@@ -586,7 +591,7 @@
             vm((ROWS, ALLCTX), F32),
             vm((4, 4 * ROWS, CH), BF),
             vm((4 * ROWS, SEGCTX), BF),
-            vm((4 * TOKL, NCOL), BF),
+            vm((2, 4 * TOKL, CH), BF),
             vm((4 * ROWS, HD), F32),
             vm((4 * ROWS, HD), F32),
             vm((4, HD, ROWS), BF),
@@ -601,9 +606,9 @@
             vm((2, 2, HD, 256), BF),
             vm((2, 2, HD, 256), BF),
             vm((2, 2, HD, CH), F32),
-            vm((6, half_w, NCOL), BF),
-            vm((6, half_w, NCOL), BF),
-            vm((2, half_w, NCOL), F32),
+            vm((6, WROWS, CH), BF),
+            vm((6, WROWS, CH), BF),
+            vm((2, WROWS, CH), F32),
             dma, dma((4,)), dma((4, 2)), dma((2, 4)), dma((2, 4)), dma((2, 4)),
             dma((6,)), dma((6,)), dma, dma, dma((6,)), dma((6,)),
             dma((6,)), dma((6,)), dma((6,)), dma((6,)), dma((6,)), dma((6,)),
@@ -612,7 +617,7 @@
         compiler_params=pltpu.CompilerParams(
             collective_id=0, has_side_effects=True, vmem_limit_bytes=VLIM),
         name="whole",
-    )(ancestors, upstream[0], advantages, out_weight, prefix_keys[0], prefix_values[0], keys[0], values[0],
+    )(ancestors[0].T, upstream[0], advantages, out_weight, prefix_keys[0], prefix_values[0], keys[0], values[0],
       queries[0])
     outs = pl.pallas_call(
         finish_kernel,

time: 113 us -> 112 us (level); the launches traced: 113 us -> 110 us
  local copies, waits for them, and re-layouts: 1.35 us -> 0 us
    unnamed x1 -> x0, local copies, waits for them, and re-layouts: 1.35 us -> none
where the time goes in v5:
time: 112 us; the launch traced here: 110 us
  Pallas kernels  110 us (98%)
    pallas_call x1, Pallas kernels, on_device(): pl.pallas_call(whole_kernel, out_shape=(sds((TOKL, NCOL), BF), sds((4, 25...  107 us
    pallas_call x1, Pallas kernels, on_device(): pl.pallas_call(finish_kernel, out_shape=tuple([sds((TOKL, NCOL), BF)] + [...  2.89 us

profile of v5, /device:TPU:0, one launch (start us, length us, event | category | flops | bytes accessed | tf_op | source)
XLA Modules:
  0.0 110.5 jit_solution(15269132753022448557)
XLA Ops:
  0.6 107.0 %whole.1 = (bf16[256,1024]{1,0:T(8,128)(2,1)}, bf16[4,256,128]{2,1,0:T(8,128)(2,1)}, f32[320,1024]{1,0:T(8,128)}) custom-call(s32[2,16]{1,0:T(2,128)} %bitcast.20, bf16[256,640]{1,0:T(8,128)(2,1)} %bitcast.15, s32[1,256]{1,0:T(1,128)} %adv.1, bf16[320,1024]{1,0:T(8,128)(2,1)} %w.1, bf16[256,128]{1,0:T(8,128)(2,1)} %bitcast.16, bf16[256,128]{1,0:T(8,128)(2,1)} %bitcast.17, ...), custom_call_target="tpu_custom_call" | custom-call | tf_op jit(solution)/shard_map/whole/pallas_call | solution.py:570
  107.6 2.9 %finish.1 = (bf16[256,1024]{1,0:T(8,128)(2,1)}, bf16[256,128]{1,0:T(8,128)(2,1)}, bf16[256,128]{1,0:T(8,128)(2,1)}, bf16[256,128]{1,0:T(8,128)(2,1)}, bf16[256,128]{1,0:T(8,128)(2,1)}, /*index=5*/f32[320,1024]{1,0:T(8,128)}) custom-call(bf16[256,1024]{1,0:T(8,128)(2,1)} %get-tuple-element.15.dq, bf16[4,256,128]{2,1,0:T(8,128)(2,1)} %get-tuple-element.16.kv, ...), custom_call_target="tpu_custom_call" | custom-call | tf_op jit(solution)/shard_map/finish/pallas_call | solution.py:622

commit v6 on v3

--- a/solution.py
+++ b/solution.py
@@ -141,7 +141,7 @@
     target_y = 2 * (x % 2) + c
     is_recv = c == y % 2
     is_src = target_y == y
-    half = x // 2
+    is_mid = is_recv & jnp.logical_not(is_src)
     sib = place(x, y, z, 1 - c)
     cexp = SCALE * LOG2E
 
@@ -165,6 +165,11 @@
     def _():
         signal(bar, xdev(1))
         signal(bar, xdev(3))
+
+    @pl.when(is_mid)
+    def _():
+        for d in range(1, 4):
+            signal(bar, place((x + 3) % 4, (y + d) % 4, z, c))
 
     rows_b = lambda b: pl.ds(pl.multiple_of(b * 256, 256), 256)
     own_rows = rows_b(y * 2 + zl)
@@ -179,7 +184,7 @@
     wview = lambda n, p: wg.at[pl.ds(pl.multiple_of(n * WROWS + p * w_half, 32), w_half)]
     wg[pl.ds(pl.multiple_of(z * WROWS, 64), WROWS), :] = w[...]
 
-    pl.semaphore_wait(bar, 6 + 2 * is_recv.astype(jnp.int32))
+    pl.semaphore_wait(bar, 6 + 2 * is_recv.astype(jnp.int32) + 1 - is_src.astype(jnp.int32))
 
     wring = GatherRing(z, zdev, wview, w_s, w_r)
     kring = GatherRing(y, ydev, lambda n, p: kvg.at[:, rows_b(n * 2 + p)], k_s, k_r)
@@ -193,43 +198,34 @@
         v = kvg.at[:, own_rows]
         return rcopy(v, v, kz_s, kz_r, place(x, y, z + 1 - 2 * zl, c))
 
-    def cy():
-        return rcopy(cot, cotb.at[half, y], c_s, c_r.at[y], place(x, target_y, z, c))
-
-    def cx(h, yy, k):
-        v = cotb.at[h, yy]
-        return rcopy(v, v, x_s.at[yy, k], x_r.at[h, yy], xdev((1, 3)[k]))
-
-    def cb(h, yy):
-        v = cotb.at[h, yy]
-        return rcopy(v, v, b_s.at[h, yy], b_r.at[h, yy], sib)
-
-    is_mid = is_recv & jnp.logical_not(is_src)
-    left_half = ((x + 3) % 4) // 2
-    right_half = ((x + 1) % 4) // 2
-
-    def mid_block(d):
-        yy = (y + d) % 4
-        cx(left_half, yy, 0).wait_recv()
-
-        @pl.when(yy < 2)
-        def _():
-            cx(left_half, yy, 0).start()
-
-        cb(left_half, yy).start()
-        cx(right_half, yy, 1).wait_recv()
-
-        @pl.when(yy >= 2)
-        def _():
-            cx(right_half, yy, 1).start()
-
-        cb(right_half, yy).start()
+    def quarter(n, yy):
+        second = (n + y // 2) % 2
+        return cotb.at[((n + 4 - second) % 4) // 2, yy, pl.ds(pl.multiple_of(second * SEG, SEG), SEG)]
+
+    def quarter_piece(n, p):
+        second = (n + y // 2) % 2
+        return cotb.at[((n + 4 - second) % 4) // 2, 2 * p:2 * p + 2, pl.ds(pl.multiple_of(second * SEG, SEG), SEG)]
+
+    xring = GatherRing(x, xdev, quarter_piece, x_s, x_r)
+
+    def cy(second):
+        dst = cotb.at[x // 2, y, second * SEG:(second + 1) * SEG]
+        return rcopy(cot.at[second * SEG:(second + 1) * SEG], dst, c_s.at[second], c_r.at[y],
+                     place((x + second) % 4, target_y, z, c))
+
+    def cy_arrived(yy):
+        rcopy(cot.at[0:SEG], quarter(x, yy), c_s.at[0], c_r.at[yy], sib).wait_recv()
+
+    def cb(n, p):
+        v = quarter_piece(n, p)
+        return rcopy(v, v, b_s.at[n, p], b_r.at[n, p], sib)
 
     kz().start()
+    cy(1).start()
 
     @pl.when(jnp.logical_not(is_src))
     def _():
-        cy().start()
+        cy(0).start()
 
     kring.send(zl)
 
@@ -245,10 +241,7 @@
 
     @pl.when(is_src)
     def _():
-        cotb[half, y] = cot[...]
-        for k in range(2):
-            cx(half, y, k).start()
-        cb(half, y).start()
+        cotb[x // 2, y, 0:SEG] = cot[0:SEG]
 
     kz().wait_recv()
     kring.send(1 - zl)
@@ -263,37 +256,37 @@
         for p in range(2):
             wring.left(p).start()
 
-    @pl.when(is_src)
-    def _():
-        for d in (1, 3, 2):
-            yy = (y + d) % 4
-            rcopy(cot, cotb.at[half, yy], c_s, c_r.at[yy], sib).wait_recv()
-            for k in range(2):
-                cx(half, yy, k).start()
-            cb(half, yy).start()
-
-    @pl.when(is_mid)
-    def _():
-        mid_block(0)
-        mid_block(1)
+    @pl.when(is_recv)
+    def _():
+        for p in range(2):
+            for yy in (2 * p, 2 * p + 1):
+                @pl.when(jnp.logical_not(is_src & (yy == y)))
+                def _():
+                    cy_arrived(yy)
+            xring.send(p)
+            cb(x, p).start()
 
     for p in range(2):
         kring.forward(p)
 
-    @pl.when(is_mid)
-    def _():
-        mid_block(3)
-        mid_block(2)
+    @pl.when(is_recv)
+    def _():
+        xring.forward(0)
+        cb((x + 3) % 4, 0).start()
+        xring.forward(1)
+        cb((x + 1) % 4, 1).start()
 
     for p in range(2):
         wring.forward(p)
     kring.wait_near()
     kring.wait_far()
 
-    named = [[jnp.broadcast_to(anc[0, pl.ds(first + s, 1), i:i + 1], (1, HD)) for i in range(2)] for s in range(2)]
+    lane = lax.broadcasted_iota(jnp.int32, (1, 16), 1)
+    named = [[jnp.broadcast_to(jnp.sum(jnp.where(lane == first + s, anc[i:i + 1, :].astype(F32), 0.0),
+                                       axis=1, keepdims=True), (1, HD)) for i in range(2)] for s in range(2)]
 
     def hot(s, i, j):
-        return (named[s][i] == j).astype(F32)
+        return (named[s][i] == float(j)).astype(F32)
 
     for s in range(2):
         own_seg = pl.ds(pl.multiple_of((first + s) * SEG, SEG), SEG)
@@ -358,11 +351,14 @@
     aring.send(0)
     forward(2)
 
-    @pl.when(is_src)
-    def _():
-        for d in (0, 1, 3, 2):
-            cx(1 - half, (y + d) % 4, 0).wait_recv()
-            cb(1 - half, (y + d) % 4).start()
+    @pl.when(is_recv)
+    def _():
+        xring.wait_near()
+        cb((x + 3) % 4, 1).start()
+        cb((x + 1) % 4, 0).start()
+        xring.wait_far()
+        for p in range(2):
+            cb((x + 2) % 4, p).start()
 
     forward(3)
     aring.send(1)
@@ -372,9 +368,9 @@
 
     @pl.when(jnp.logical_not(is_recv))
     def _():
-        for h in range(2):
-            for yy in range(4):
-                cb(h, yy).wait_recv()
+        for n in range(4):
+            for p in range(2):
+                cb(n, p).wait_recv()
 
     def proj(yy, rows):
         return jnp.dot(cotb[0, yy, rows, :], wg[0:UCOL, :], preferred_element_type=F32) + jnp.dot(
@@ -463,6 +459,8 @@
             segt[y, k, :, own_cols] += accs[s, k, :, 2 * SEG:]
     rring.send(0, segt[(y + 2) % 4])
     rring.send(3, segt[(y + 3) % 4])
+    gring.add_send(4, gnear[0])
+    gring.add_send(5, gnear[1])
 
     def prefix(j):
         acc[...] = jnp.zeros_like(acc)
@@ -478,8 +476,6 @@
 
     prefix((y + 2) % 4)
     rring.send(1, acc[...])
-    gring.add_send(4, gnear[0])
-    gring.add_send(5, gnear[1])
     rring.add_send(4, segt[(y + 1) % 4])
     prefix((y + 1) % 4)
     rring.send(2, acc[...])
@@ -524,26 +520,18 @@
     for p in range(2):
         zk(p).wait_send()
 
+    cy(1).wait_send()
+
     @pl.when(jnp.logical_not(is_src))
     def _():
-        cy().wait_send()
-
-    @pl.when(is_src)
-    def _():
-        for yy in range(4):
-            for k in range(2):
-                cx(half, yy, k).wait_send()
-
-    @pl.when(is_mid)
-    def _():
-        for yy in range(4):
-            cx(0, yy, yy // 2).wait_send()
+        cy(0).wait_send()
 
     @pl.when(is_recv)
     def _():
-        for h in range(2):
-            for yy in range(4):
-                cb(h, yy).wait_send()
+        xring.wait_sends()
+        for n in range(4):
+            for p in range(2):
+                cb(n, p).wait_send()
 
     for ring in (wring, kring, aring, dring, rring, gring):
         ring.wait_sends()
@@ -605,7 +593,7 @@
             vm((6, half_w, NCOL), BF),
             vm((6, half_w, NCOL), BF),
             vm((2, half_w, NCOL), F32),
-            dma, dma((4,)), dma((4, 2)), dma((2, 4)), dma((2, 4)), dma((2, 4)),
+            dma((2,)), dma((4,)), dma((6,)), dma((6,)), dma((4, 2)), dma((4, 2)),
             dma((6,)), dma((6,)), dma, dma, dma((6,)), dma((6,)),
             dma((6,)), dma((6,)), dma((6,)), dma((6,)), dma((6,)), dma((6,)),
             dma((2,)), dma((2,)), dma((6,)), dma((6,)),
@@ -613,7 +601,7 @@
         compiler_params=pltpu.CompilerParams(
             collective_id=0, has_side_effects=True, vmem_limit_bytes=VLIM),
         name="whole",
-    )(ancestors, upstream[0], advantages, out_weight, prefix_keys[0], prefix_values[0], keys[0], values[0],
+    )(ancestors[0].T, upstream[0], advantages, out_weight, prefix_keys[0], prefix_values[0], keys[0], values[0],
       queries[0])
     outs = pl.pallas_call(
         finish_kernel,

time: 107 us -> 104 us (0.972)
  Pallas kernels: 105 us -> 102 us
  local copies, waits for them, and re-layouts: 1.35 us -> 0 us
    pallas_call x1, Pallas kernels: 102 us -> 99.6 us  [on_device(): pl.pallas_call(whole_kernel, out_shape=(sds((TOKL, NCOL), BF), sds((4, 25...]
    unnamed x1 -> x0, local copies, waits for them, and re-layouts: 1.35 us -> none
where the time goes in v6:
time: 104 us; the launch traced here: 103 us
  Pallas kernels  102 us (98%)
    pallas_call x1, Pallas kernels, on_device(): pl.pallas_call(whole_kernel, out_shape=(sds((TOKL, NCOL), BF), sds((4, 25...  99.6 us
    pallas_call x1, Pallas kernels, on_device(): pl.pallas_call(finish_kernel, out_shape=tuple([sds((TOKL, NCOL), BF)] + [...  2.89 us

profile of v6, /device:TPU:0, one launch (start us, length us, event | category | flops | bytes accessed | tf_op | source)
XLA Modules:
  0.0 103.1 jit_solution(12923054886471436032)
XLA Ops:
  0.6 99.6 %whole.1 = (bf16[256,1024]{1,0:T(8,128)(2,1)}, bf16[4,256,128]{2,1,0:T(8,128)(2,1)}, f32[320,1024]{1,0:T(8,128)}) custom-call(s32[2,16]{1,0:T(2,128)} %bitcast.20, bf16[256,640]{1,0:T(8,128)(2,1)} %bitcast.15, s32[1,256]{1,0:T(1,128)} %adv.1, bf16[320,1024]{1,0:T(8,128)(2,1)} %w.1, bf16[256,128]{1,0:T(8,128)(2,1)} %bitcast.16, bf16[256,128]{1,0:T(8,128)(2,1)} %bitcast.17, ...), custom_call_target="tpu_custom_call" | custom-call | tf_op jit(solution)/shard_map/whole/pallas_call | solution.py:554
  100.2 2.9 %finish.1 = (bf16[256,1024]{1,0:T(8,128)(2,1)}, bf16[256,128]{1,0:T(8,128)(2,1)}, bf16[256,128]{1,0:T(8,128)(2,1)}, bf16[256,128]{1,0:T(8,128)(2,1)}, bf16[256,128]{1,0:T(8,128)(2,1)}, /*index=5*/f32[320,1024]{1,0:T(8,128)}) custom-call(bf16[256,1024]{1,0:T(8,128)(2,1)} %get-tuple-element.15.dq, bf16[4,256,128]{2,1,0:T(8,128)(2,1)} %get-tuple-element.16.kv, ...), custom_call_target="tpu_custom_call" | custom-call | tf_op jit(solution)/shard_map/finish/pallas_call | solution.py:606

commit v7 on v6

--- a/solution.py
+++ b/solution.py
@@ -276,9 +276,72 @@
         xring.forward(1)
         cb((x + 1) % 4, 1).start()
 
-    for p in range(2):
-        wring.forward(p)
+    @pl.when(zl == 0)
+    def _():
+        wring.forward(0)
+
+    @pl.when(zl == 1)
+    def _():
+        wring.forward(1)
+
     kring.wait_near()
+    nh = ROWS // SEG
+
+    def spot(rb):
+        s, hb = rb // 2, rb % 2
+        return s, hb, slice(s * SEG, (s + 1) * SEG), slice(rb * ROWS, (rb + 1) * ROWS), [
+            slice((hb * nh + i) * HD, (hb * nh + i + 1) * HD) for i in range(nh)]
+
+    def crow(j):
+        return pl.ds(pl.multiple_of(j * CH, CH), CH)
+
+    def lane_max(sc, mx):
+        for t in range(sc.shape[1] // HD):
+            part = sc[:, t * HD:(t + 1) * HD]
+            mx = part if mx is None else jnp.maximum(mx, part)
+        return mx
+
+    def lane_sum(p, tot):
+        for t in range(p.shape[1] // HD):
+            part = p[:, t * HD:(t + 1) * HD]
+            tot = part if tot is None else tot + part
+        return tot
+
+    def forward_near(rb):
+        s, hb, tok, rows, heads = spot(rb)
+        qb = jnp.concatenate([q[tok, h] for h in heads], axis=0)
+        qt[rb] = qb.T
+        mx = None
+        for i, d in enumerate((0, 1, 3)):
+            sc = nt_dot(qb, kvg[0, crow((y + d) % 4), :])
+            s_f[:, i * CH:(i + 1) * CH] = sc
+            mx = lane_max(sc, mx)
+        m = jnp.max(mx, axis=1, keepdims=True)
+        lsum = None
+        o = None
+        for i, d in enumerate((0, 1, 3)):
+            j = (y + d) % 4
+            p = jnp.exp2((s_f[:, i * CH:(i + 1) * CH] - m) * cexp)
+            lsum = lane_sum(p, lsum)
+            pb = p.astype(BF)
+            p_b[j, rows, :] = pb
+            oc = jnp.dot(pb, kvg[1, crow(j), :], preferred_element_type=F32)
+            o = oc if o is None else o + oc
+        delta[0, rows, :] = lsum
+        delta[1, rows, :] = jnp.broadcast_to(m, (ROWS, HD))
+        dqa[rows, :] = o
+
+    for rb in range(4):
+        forward_near(rb)
+
+    @pl.when(zl == 0)
+    def _():
+        wring.forward(1)
+
+    @pl.when(zl == 1)
+    def _():
+        wring.forward(0)
+
     kring.wait_far()
 
     lane = lax.broadcasted_iota(jnp.int32, (1, 16), 1)
@@ -294,62 +357,54 @@
             for i in range(2):
                 tot = None
                 for j in range(16):
-                    v = kvg[2 + k, j * SEG:(j + 1) * SEG, :].astype(F32) * hot(s, i, j)
+                    v = kvg[2 + k, j * SEG:(j + 1) * SEG, :] * hot(s, i, j).astype(BF)
                     tot = v if tot is None else tot + v
-                dst[s, i * SEG:(i + 1) * SEG, :] = tot.astype(BF)
+                dst[s, i * SEG:(i + 1) * SEG, :] = tot
             dst[s, 2 * SEG:, :] = kvg[2 + k, own_seg, :]
 
-    nh = ROWS // SEG
-
-    def forward(rb):
-        s, hb = rb // 2, rb % 2
-        tok = slice(s * SEG, (s + 1) * SEG)
-        rows = slice(rb * ROWS, (rb + 1) * ROWS)
+    def forward_far(rb):
+        s, hb, tok, rows, heads = spot(rb)
         col = lax.broadcasted_iota(jnp.int32, (ROWS, SEG), 1)
         row = lax.broadcasted_iota(jnp.int32, (ROWS, SEG), 0) % SEG
         shut = [jnp.where(named[s][i] >= 0, 0.0, -1e30) for i in range(2)]
         shut.append(jnp.where(col <= row, 0.0, -1e30))
-        heads = [slice((hb * nh + i) * HD, (hb * nh + i + 1) * HD) for i in range(nh)]
         qb = jnp.concatenate([q[tok, h] for h in heads], axis=0)
-        qt[rb] = qb.T
-        mx = None
-        for j in range(5):
-            kc = kvg[0, j * CH:(j + 1) * CH, :] if j < 4 else kcs[s]
-            sc = nt_dot(qb, kc)
-            n = sc.shape[1]
-            if j == 4:
-                sc = jnp.concatenate([sc[:, i * SEG:(i + 1) * SEG] + shut[i] for i in range(3)], axis=1)
-            s_f[:, j * CH:j * CH + n] = sc
-            for t in range(n // 128):
-                part = sc[:, t * 128:(t + 1) * 128]
-                mx = part if mx is None else jnp.maximum(mx, part)
-        m = jnp.max(mx, axis=1, keepdims=True)
-        lsum = None
-        o = None
-        for j in range(5):
-            vc = kvg[1, j * CH:(j + 1) * CH, :] if j < 4 else vcs[s]
-            n = vc.shape[0]
-            p = jnp.exp2((s_f[:, j * CH:j * CH + n] - m) * cexp)
-            for t in range(n // 128):
-                part = p[:, t * 128:(t + 1) * 128]
-                lsum = part if lsum is None else lsum + part
-            pb = p.astype(BF)
-            if j < 4:
-                p_b[j, rows, :] = pb
-            else:
-                p_s[rows, :] = pb
-            oc = jnp.dot(pb, vc, preferred_element_type=F32)
-            o = oc if o is None else o + oc
+        far = (y + 2) % 4
+        sc = nt_dot(qb, kvg[0, crow(far), :])
+        s_f[:, 0:CH] = sc
+        mx = lane_max(sc, None)
+        sc = nt_dot(qb, kcs[s])
+        sc = jnp.concatenate([sc[:, i * SEG:(i + 1) * SEG] + shut[i] for i in range(3)], axis=1)
+        s_f[:, CH:CH + SEGCTX] = sc
+        mx = lane_max(sc, mx)
+        m_near = delta[1, rows, 0:1]
+        m = jnp.maximum(jnp.max(mx, axis=1, keepdims=True), m_near)
+        p = jnp.exp2((s_f[:, 0:CH] - m) * cexp)
+        lsum = lane_sum(p, None)
+        pb = p.astype(BF)
+        p_b[far, rows, :] = pb
+        o = jnp.dot(pb, kvg[1, crow(far), :], preferred_element_type=F32)
+        p = jnp.exp2((s_f[:, CH:CH + SEGCTX] - m) * cexp)
+        lsum = lane_sum(p, lsum)
+        pb = p.astype(BF)
+        p_s[rows, :] = pb
+        o = o + jnp.dot(pb, vcs[s], preferred_element_type=F32)
+        ratio = jnp.broadcast_to(jnp.exp2((m_near - m) * cexp), (ROWS, HD))
+        lsum = lsum + delta[0, rows, :] * ratio
+        o = o + dqa[rows, :] * ratio
         il = jnp.broadcast_to(1.0 / jnp.sum(lsum, axis=1, keepdims=True), (ROWS, HD))
-        il_b[rows, :] = il
+        il_b[0, rows, :] = il
+        il_b[1, rows, :] = il * ratio
         ob = (o * il).astype(BF)
         for i, h in enumerate(heads):
             attng[pl.ds(pl.multiple_of(y * TOKL + s * SEG, SEG), SEG), h] = ob[i * SEG:(i + 1) * SEG]
 
-    forward(0)
-    forward(1)
+    forward_far(0)
+    forward_far(1)
     aring.send(0)
-    forward(2)
+    forward_far(2)
+    forward_far(3)
+    aring.send(1)
 
     @pl.when(is_recv)
     def _():
@@ -359,9 +414,6 @@
         xring.wait_far()
         for p in range(2):
             cb((x + 2) % 4, p).start()
-
-    forward(3)
-    aring.send(1)
 
     wring.wait_near()
     wring.wait_far()
@@ -411,34 +463,48 @@
     dring.wait_result()
     for p in range(2):
         dattn[p * SEG:(p + 1) * SEG, :] = dring.result(p, dnear[2 + p]).astype(BF)
-    for rb in range(4):
-        s, hb = rb // 2, rb % 2
-        rows = slice(rb * ROWS, (rb + 1) * ROWS)
-        tok = slice(s * SEG, (s + 1) * SEG)
-        arow = pl.ds(pl.multiple_of(y * TOKL + s * SEG, SEG), SEG)
-        heads = [slice((hb * nh + i) * HD, (hb * nh + i + 1) * HD) for i in range(nh)]
-        dob = jnp.concatenate([dattn[tok, h] for h in heads], axis=0)
-        at = jnp.concatenate([attng[arow, h] for h in heads], axis=0)
-        db = (dob.astype(F32) * il_b[rows, :]).astype(BF)
-        dos[rows, :] = db
-        dost[rb] = db.T
-        dl = jnp.sum(db.astype(F32) * at.astype(F32), axis=1, keepdims=True)
-        delta[rows, :] = jnp.broadcast_to(dl, (ROWS, HD))
-
-    def back(rb, kc, vc, pb):
+    def scale_grads(g):
+        for rb in range(4):
+            s, hb, tok, rows, heads = spot(rb)
+            arow = pl.ds(pl.multiple_of(y * TOKL + s * SEG, SEG), SEG)
+            dob = jnp.concatenate([dattn[tok, h] for h in heads], axis=0)
+            at = jnp.concatenate([attng[arow, h] for h in heads], axis=0)
+            db = (dob.astype(F32) * il_b[g, rows, :]).astype(BF)
+            dos[g, rows, :] = db
+            dost[g, rb] = db.T
+            dl = jnp.sum(db.astype(F32) * at.astype(F32), axis=1, keepdims=True)
+            delta[g, rows, :] = jnp.broadcast_to(dl, (ROWS, HD))
+
+    def back(g, rb, kc, vc, pb):
         rows = pl.ds(pl.multiple_of(rb * ROWS, ROWS), ROWS)
-        dl = delta[rows, :]
+        dl = delta[g, rows, :]
         n = vc.shape[0]
-        dp = nt_dot(dos[rows, :], vc)
+        dp = nt_dot(dos[g, rows, :], vc)
         ds = (pb.astype(F32) * (dp - jnp.concatenate([dl] * (n // HD), axis=1))).astype(BF)
         return (rows, jnp.dot(ds, kc, preferred_element_type=F32),
                 jnp.dot(qt[rb], ds, preferred_element_type=F32),
-                jnp.dot(dost[rb], pb, preferred_element_type=F32))
+                jnp.dot(dost[g, rb], pb, preferred_element_type=F32))
+
+    def prefix(g, j):
+        acc[...] = jnp.zeros_like(acc)
+
+        @pl.loop(0, 4)
+        def _(rb):
+            rows = pl.ds(pl.multiple_of(rb * ROWS, ROWS), ROWS)
+            _, dqc, dk, dv = back(g, rb, kvg[0, crow(j), :], kvg[1, crow(j), :], p_b[j, rows, :])
+            dqa[rows, :] += dqc
+            acc[0] += dk
+            acc[1] += dv
+
+    scale_grads(0)
+    dqa[...] = jnp.zeros_like(dqa)
+    prefix(0, (y + 2) % 4)
+    rring.send(1, acc[...])
 
     for rb in range(4):
         s = rb // 2
-        rows, dqc, dk, dv = back(rb, kcs[s], vcs[s], p_s[rb * ROWS:(rb + 1) * ROWS, :])
-        dqa[rows, :] = dqc
+        rows, dqc, dk, dv = back(0, rb, kcs[s], vcs[s], p_s[rb * ROWS:(rb + 1) * ROWS, :])
+        dqa[rows, :] += dqc
         if rb % 2 == 0:
             accs[s, 0] = dk
             accs[s, 1] = dv
@@ -462,26 +528,13 @@
     gring.add_send(4, gnear[0])
     gring.add_send(5, gnear[1])
 
-    def prefix(j):
-        acc[...] = jnp.zeros_like(acc)
-        crow = pl.ds(pl.multiple_of(j * CH, CH), CH)
-
-        @pl.loop(0, 4)
-        def _(rb):
-            rows = pl.ds(pl.multiple_of(rb * ROWS, ROWS), ROWS)
-            _, dqc, dk, dv = back(rb, kvg[0, crow, :], kvg[1, crow, :], p_b[j, rows, :])
-            dqa[rows, :] += dqc
-            acc[0] += dk
-            acc[1] += dv
-
-    prefix((y + 2) % 4)
-    rring.send(1, acc[...])
+    scale_grads(1)
+    prefix(1, (y + 1) % 4)
+    rring.send(2, acc[...])
     rring.add_send(4, segt[(y + 1) % 4])
-    prefix((y + 1) % 4)
-    rring.send(2, acc[...])
-    prefix((y + 3) % 4)
+    prefix(1, (y + 3) % 4)
     rring.add_send(5, acc[...])
-    prefix(y)
+    prefix(1, y)
     for rb in range(4):
         s, hb = rb // 2, rb % 2
         dqb = (dqa[rb * ROWS:(rb + 1) * ROWS, :] * SCALE).astype(BF)
@@ -572,15 +625,15 @@
             vm((6, SEG, NCOL), BF),
             vm((4, SEG, NCOL), F32),
             vm((TOKL, NCOL), BF),
-            vm((ROWS, ALLCTX), F32),
+            vm((ROWS, 3 * CH), F32),
             vm((4, 4 * ROWS, CH), BF),
             vm((4 * ROWS, SEGCTX), BF),
             vm((4 * TOKL, NCOL), BF),
-            vm((4 * ROWS, HD), F32),
-            vm((4 * ROWS, HD), F32),
+            vm((2, 4 * ROWS, HD), F32),
+            vm((2, 4 * ROWS, HD), F32),
             vm((4, HD, ROWS), BF),
-            vm((4 * ROWS, HD), BF),
-            vm((4, HD, ROWS), BF),
+            vm((2, 4 * ROWS, HD), BF),
+            vm((2, 4, HD, ROWS), BF),
             vm((4 * ROWS, HD), F32),
             vm((2, HD, CH), F32),
             vm((2, 2, HD, SEGCTX), F32),

time: 104 us -> 106 us (1.019)
  Pallas kernels: 102 us -> 105 us
    pallas_call x1, Pallas kernels: 99.6 us -> 102 us  [on_device(): pl.pallas_call(whole_kernel, out_shape=(sds((TOKL, NCOL), BF), sds((4, 25...]
where the time goes in v7:
time: 106 us
  Pallas kernels  105 us (99%)
    pallas_call x1, Pallas kernels, on_device(): pl.pallas_call(whole_kernel, out_shape=(sds((TOKL, NCOL), BF), sds((4, 25...  102 us
    pallas_call x1, Pallas kernels, on_device(): pl.pallas_call(finish_kernel, out_shape=tuple([sds((TOKL, NCOL), BF)] + [...  2.89 us

profile of v7, /device:TPU:0, one launch (start us, length us, event | category | flops | bytes accessed | tf_op | source)
XLA Modules:
  0.0 105.7 jit_solution(3788694328348969006)
XLA Ops:
  0.6 102.2 %whole.1 = (bf16[256,1024]{1,0:T(8,128)(2,1)}, bf16[4,256,128]{2,1,0:T(8,128)(2,1)}, f32[320,1024]{1,0:T(8,128)}) custom-call(s32[2,16]{1,0:T(2,128)} %bitcast.20, bf16[256,640]{1,0:T(8,128)(2,1)} %bitcast.15, s32[1,256]{1,0:T(1,128)} %adv.1, bf16[320,1024]{1,0:T(8,128)(2,1)} %w.1, bf16[256,128]{1,0:T(8,128)(2,1)} %bitcast.16, bf16[256,128]{1,0:T(8,128)(2,1)} %bitcast.17, ...), custom_call_target="tpu_custom_call" | custom-call | tf_op jit(solution)/shard_map/whole/pallas_call | solution.py:607
  102.8 2.9 %finish.1 = (bf16[256,1024]{1,0:T(8,128)(2,1)}, bf16[256,128]{1,0:T(8,128)(2,1)}, bf16[256,128]{1,0:T(8,128)(2,1)}, bf16[256,128]{1,0:T(8,128)(2,1)}, bf16[256,128]{1,0:T(8,128)(2,1)}, /*index=5*/f32[320,1024]{1,0:T(8,128)}) custom-call(bf16[256,1024]{1,0:T(8,128)(2,1)} %get-tuple-element.15.dq, bf16[4,256,128]{2,1,0:T(8,128)(2,1)} %get-tuple-element.16.kv, ...), custom_call_target="tpu_custom_call" | custom-call | tf_op jit(solution)/shard_map/finish/pallas_call | solution.py:659

commit v8 on v7

--- a/solution.py
+++ b/solution.py
@@ -393,8 +393,8 @@
         lsum = lsum + delta[0, rows, :] * ratio
         o = o + dqa[rows, :] * ratio
         il = jnp.broadcast_to(1.0 / jnp.sum(lsum, axis=1, keepdims=True), (ROWS, HD))
-        il_b[0, rows, :] = il
-        il_b[1, rows, :] = il * ratio
+        il_b[rows, :] = il
+        delta[1, rows, :] = ratio
         ob = (o * il).astype(BF)
         for i, h in enumerate(heads):
             attng[pl.ds(pl.multiple_of(y * TOKL + s * SEG, SEG), SEG), h] = ob[i * SEG:(i + 1) * SEG]
@@ -414,6 +414,8 @@
         xring.wait_far()
         for p in range(2):
             cb((x + 2) % 4, p).start()
+
+    aring.forward(0)
 
     wring.wait_near()
     wring.wait_far()
@@ -438,11 +440,15 @@
     dnear[2] = proj(y, lo)
     dnear[3] = proj(y, hi)
 
+    aring.forward(1)
     for h in range(2):
         for yy in range(4):
             cott[h * UCOL:(h + 1) * UCOL, yy * TOKL:(yy + 1) * TOKL] = cotb[h, yy].T
-    for p in range(2):
-        aring.forward(p)
+    for d in (0, 1, 3):
+        for rb in range(4):
+            j, rows = (y + d) % 4, slice(rb * ROWS, (rb + 1) * ROWS)
+            ratio = jnp.concatenate([delta[1, rows, :]] * (CH // HD), axis=1)
+            p_b[j, rows, :] = (p_b[j, rows, :].astype(F32) * ratio).astype(BF)
     dring.add_send(4, dnear[0])
     dring.add_send(5, dnear[1])
 
@@ -463,48 +469,42 @@
     dring.wait_result()
     for p in range(2):
         dattn[p * SEG:(p + 1) * SEG, :] = dring.result(p, dnear[2 + p]).astype(BF)
-    def scale_grads(g):
-        for rb in range(4):
-            s, hb, tok, rows, heads = spot(rb)
-            arow = pl.ds(pl.multiple_of(y * TOKL + s * SEG, SEG), SEG)
-            dob = jnp.concatenate([dattn[tok, h] for h in heads], axis=0)
-            at = jnp.concatenate([attng[arow, h] for h in heads], axis=0)
-            db = (dob.astype(F32) * il_b[g, rows, :]).astype(BF)
-            dos[g, rows, :] = db
-            dost[g, rb] = db.T
-            dl = jnp.sum(db.astype(F32) * at.astype(F32), axis=1, keepdims=True)
-            delta[g, rows, :] = jnp.broadcast_to(dl, (ROWS, HD))
-
-    def back(g, rb, kc, vc, pb):
+    for rb in range(4):
+        s, hb, tok, rows, heads = spot(rb)
+        arow = pl.ds(pl.multiple_of(y * TOKL + s * SEG, SEG), SEG)
+        dob = jnp.concatenate([dattn[tok, h] for h in heads], axis=0)
+        at = jnp.concatenate([attng[arow, h] for h in heads], axis=0)
+        db = (dob.astype(F32) * il_b[rows, :]).astype(BF)
+        dos[rows, :] = db
+        dost[rb] = db.T
+        dl = jnp.sum(db.astype(F32) * at.astype(F32), axis=1, keepdims=True)
+        delta[0, rows, :] = jnp.broadcast_to(dl, (ROWS, HD))
+
+    def back(rb, kc, vc, pb):
         rows = pl.ds(pl.multiple_of(rb * ROWS, ROWS), ROWS)
-        dl = delta[g, rows, :]
+        dl = delta[0, rows, :]
         n = vc.shape[0]
-        dp = nt_dot(dos[g, rows, :], vc)
+        dp = nt_dot(dos[rows, :], vc)
         ds = (pb.astype(F32) * (dp - jnp.concatenate([dl] * (n // HD), axis=1))).astype(BF)
         return (rows, jnp.dot(ds, kc, preferred_element_type=F32),
                 jnp.dot(qt[rb], ds, preferred_element_type=F32),
-                jnp.dot(dost[g, rb], pb, preferred_element_type=F32))
-
-    def prefix(g, j):
+                jnp.dot(dost[rb], pb, preferred_element_type=F32))
+
+    def prefix(j):
         acc[...] = jnp.zeros_like(acc)
 
         @pl.loop(0, 4)
         def _(rb):
             rows = pl.ds(pl.multiple_of(rb * ROWS, ROWS), ROWS)
-            _, dqc, dk, dv = back(g, rb, kvg[0, crow(j), :], kvg[1, crow(j), :], p_b[j, rows, :])
+            _, dqc, dk, dv = back(rb, kvg[0, crow(j), :], kvg[1, crow(j), :], p_b[j, rows, :])
             dqa[rows, :] += dqc
             acc[0] += dk
             acc[1] += dv
 
-    scale_grads(0)
-    dqa[...] = jnp.zeros_like(dqa)
-    prefix(0, (y + 2) % 4)
-    rring.send(1, acc[...])
-
     for rb in range(4):
         s = rb // 2
-        rows, dqc, dk, dv = back(0, rb, kcs[s], vcs[s], p_s[rb * ROWS:(rb + 1) * ROWS, :])
-        dqa[rows, :] += dqc
+        rows, dqc, dk, dv = back(rb, kcs[s], vcs[s], p_s[rb * ROWS:(rb + 1) * ROWS, :])
+        dqa[rows, :] = dqc
         if rb % 2 == 0:
             accs[s, 0] = dk
             accs[s, 1] = dv
@@ -528,13 +528,14 @@
     gring.add_send(4, gnear[0])
     gring.add_send(5, gnear[1])
 
-    scale_grads(1)
-    prefix(1, (y + 1) % 4)
+    prefix((y + 2) % 4)
+    rring.send(1, acc[...])
+    prefix((y + 1) % 4)
     rring.send(2, acc[...])
     rring.add_send(4, segt[(y + 1) % 4])
-    prefix(1, (y + 3) % 4)
+    prefix((y + 3) % 4)
     rring.add_send(5, acc[...])
-    prefix(1, y)
+    prefix(y)
     for rb in range(4):
         s, hb = rb // 2, rb % 2
         dqb = (dqa[rb * ROWS:(rb + 1) * ROWS, :] * SCALE).astype(BF)
@@ -629,11 +630,11 @@
             vm((4, 4 * ROWS, CH), BF),
             vm((4 * ROWS, SEGCTX), BF),
             vm((4 * TOKL, NCOL), BF),
-            vm((2, 4 * ROWS, HD), F32),
+            vm((4 * ROWS, HD), F32),
             vm((2, 4 * ROWS, HD), F32),
             vm((4, HD, ROWS), BF),
-            vm((2, 4 * ROWS, HD), BF),
-            vm((2, 4, HD, ROWS), BF),
+            vm((4 * ROWS, HD), BF),
+            vm((4, HD, ROWS), BF),
             vm((4 * ROWS, HD), F32),
             vm((2, HD, CH), F32),
             vm((2, 2, HD, SEGCTX), F32),

time: 106 us -> 104 us (0.981)
  the two profiles are of different devices: /device:TPU:0 before, /device:TPU:34 now
where the time goes in v8:
time: 104 us; the launch traced here: 103 us
  Pallas kernels  103 us (99%)
    pallas_call x1, Pallas kernels, on_device(): pl.pallas_call(whole_kernel, out_shape=(sds((TOKL, NCOL), BF), sds((4, 25...  100 us
    pallas_call x1, Pallas kernels, on_device(): pl.pallas_call(finish_kernel, out_shape=tuple([sds((TOKL, NCOL), BF)] + [...  2.89 us

profile of v8, /device:TPU:34, one launch (start us, length us, event | category | flops | bytes accessed | tf_op | source)
XLA Modules:
  0.0 103.5 jit_solution(9871713418651335954)
XLA Ops:
  0.6 100.0 %whole.1 = (bf16[256,1024]{1,0:T(8,128)(2,1)}, bf16[4,256,128]{2,1,0:T(8,128)(2,1)}, f32[320,1024]{1,0:T(8,128)}) custom-call(s32[2,16]{1,0:T(2,128)} %bitcast.20, bf16[256,640]{1,0:T(8,128)(2,1)} %bitcast.15, s32[1,256]{1,0:T(1,128)} %adv.1, bf16[320,1024]{1,0:T(8,128)(2,1)} %w.1, bf16[256,128]{1,0:T(8,128)(2,1)} %bitcast.16, bf16[256,128]{1,0:T(8,128)(2,1)} %bitcast.17, ...), custom_call_target="tpu_custom_call" | custom-call | tf_op jit(solution)/shard_map/whole/pallas_call | solution.py:608
  100.6 2.9 %finish.1 = (bf16[256,1024]{1,0:T(8,128)(2,1)}, bf16[256,128]{1,0:T(8,128)(2,1)}, bf16[256,128]{1,0:T(8,128)(2,1)}, bf16[256,128]{1,0:T(8,128)(2,1)}, bf16[256,128]{1,0:T(8,128)(2,1)}, /*index=5*/f32[320,1024]{1,0:T(8,128)}) custom-call(bf16[256,1024]{1,0:T(8,128)(2,1)} %get-tuple-element.15.dq, bf16[4,256,128]{2,1,0:T(8,128)(2,1)} %get-tuple-element.16.kv, ...), custom_call_target="tpu_custom_call" | custom-call | tf_op jit(solution)/shard_map/finish/pallas_call | solution.py:660

commit v9 on v8

--- a/solution.py
+++ b/solution.py
@@ -191,7 +191,8 @@
     aring = GatherRing(
         y, ydev, lambda n, p: attng.at[pl.ds(pl.multiple_of(n * TOKL + p * SEG, SEG), SEG)], a_s, a_r)
     dring = SumRing(ydev, dsb, drb, d_s, d_r)
-    rring = SumRing(ydev, ksb, krb, r_s, r_r)
+    pring = SumRing(ydev, ksb.at[0], krb.at[0], r_s.at[0], r_r.at[0])
+    sring = SumRing(ydev, ksb.at[1], krb.at[1], r_s.at[1], r_r.at[1])
     gring = SumRing(zdev, gsb, grb, g_s, g_r)
 
     def kz():
@@ -466,6 +467,7 @@
     gnear[0] = wgrad((z + 1) % 4, 0)
     gnear[1] = wgrad((z + 3) % 4, 1)
 
+    dqa[...] = jnp.zeros_like(dqa)
     dring.wait_result()
     for p in range(2):
         dattn[p * SEG:(p + 1) * SEG, :] = dring.result(p, dnear[2 + p]).astype(BF)
@@ -501,10 +503,14 @@
             acc[0] += dk
             acc[1] += dv
 
+    prefix((y + 2) % 4)
+    for k in range(2):
+        pring.send(k, acc[k])
+
     for rb in range(4):
         s = rb // 2
         rows, dqc, dk, dv = back(rb, kcs[s], vcs[s], p_s[rb * ROWS:(rb + 1) * ROWS, :])
-        dqa[rows, :] = dqc
+        dqa[rows, :] += dqc
         if rb % 2 == 0:
             accs[s, 0] = dk
             accs[s, 1] = dv
@@ -523,18 +529,21 @@
         own_cols = pl.ds(pl.multiple_of((zl * 2 + s) * SEG, SEG), SEG)
         for k in range(2):
             segt[y, k, :, own_cols] += accs[s, k, :, 2 * SEG:]
-    rring.send(0, segt[(y + 2) % 4])
-    rring.send(3, segt[(y + 3) % 4])
+    for k in range(2):
+        sring.send(k, segt[(y + 2) % 4, k])
+    sring.send(2, segt[(y + 1) % 4, 1])
+    sring.send(3, segt[(y + 3) % 4, 0])
     gring.add_send(4, gnear[0])
     gring.add_send(5, gnear[1])
 
-    prefix((y + 2) % 4)
-    rring.send(1, acc[...])
     prefix((y + 1) % 4)
-    rring.send(2, acc[...])
-    rring.add_send(4, segt[(y + 1) % 4])
+    pring.send(2, acc[1])
+    pring.add_send(4, acc[0])
+    sring.add_send(4, segt[(y + 1) % 4, 0])
+    sring.add_send(5, segt[(y + 3) % 4, 1])
     prefix((y + 3) % 4)
-    rring.add_send(5, acc[...])
+    pring.send(3, acc[0])
+    pring.add_send(5, acc[1])
     prefix(y)
     for rb in range(4):
         s, hb = rb // 2, rb % 2
@@ -551,9 +560,10 @@
         return rcopy(zsb.at[p], zrb.at[p], zk_s.at[p], zk_r.at[p], place(x, y, z + 1 - 2 * zl, c))
 
     for p in range(2):
-        for i in ((4, 3), (2, 5))[p]:
-            rring.copy(i).wait_recv()
-        kown[p] = rring.result(p, segt[y] if p == 0 else acc[...])
+        ring = (sring, pring)[p]
+        ring.wait_result()
+        for k in range(2):
+            kown[p, k] = ring.result(k, segt[y, k] if p == 0 else acc[k])
         zsb[p] = kown[p, :, :, lanes(1 - zl)].astype(BF)
         zk(p).start()
 
@@ -587,7 +597,7 @@
             for p in range(2):
                 cb(n, p).wait_send()
 
-    for ring in (wring, kring, aring, dring, rring, gring):
+    for ring in (wring, kring, aring, dring, pring, sring, gring):
         ring.wait_sends()
 
 
@@ -639,8 +649,8 @@
             vm((2, HD, CH), F32),
             vm((2, 2, HD, SEGCTX), F32),
             vm((4, 2, HD, CH), F32),
-            vm((6, 2, HD, CH), BF),
-            vm((6, 2, HD, CH), BF),
+            vm((2, 6, HD, CH), BF),
+            vm((2, 6, HD, CH), BF),
             vm((2, 2, HD, 256), BF),
             vm((2, 2, HD, 256), BF),
             vm((2, 2, HD, CH), F32),
@@ -649,7 +659,7 @@
             vm((2, half_w, NCOL), F32),
             dma((2,)), dma((4,)), dma((6,)), dma((6,)), dma((4, 2)), dma((4, 2)),
             dma((6,)), dma((6,)), dma, dma, dma((6,)), dma((6,)),
-            dma((6,)), dma((6,)), dma((6,)), dma((6,)), dma((6,)), dma((6,)),
+            dma((6,)), dma((6,)), dma((6,)), dma((6,)), dma((2, 6)), dma((2, 6)),
             dma((2,)), dma((2,)), dma((6,)), dma((6,)),
         ],
         compiler_params=pltpu.CompilerParams(

time: 104 us -> 104 us (level)
  the two profiles are of different devices: /device:TPU:34 before, /device:TPU:0 now
where the time goes in v9:
time: 104 us
  Pallas kernels  103 us (99%)
    pallas_call x1, Pallas kernels, on_device(): pl.pallas_call(whole_kernel, out_shape=(sds((TOKL, NCOL), BF), sds((4, 25...  100 us
    pallas_call x1, Pallas kernels, on_device(): pl.pallas_call(finish_kernel, out_shape=tuple([sds((TOKL, NCOL), BF)] + [...  2.89 us

profile of v9, /device:TPU:0, one launch (start us, length us, event | category | flops | bytes accessed | tf_op | source)
XLA Modules:
  0.0 104.0 jit_solution(16796723664821692014)
XLA Ops:
  0.6 100.4 %whole.1 = (bf16[256,1024]{1,0:T(8,128)(2,1)}, bf16[4,256,128]{2,1,0:T(8,128)(2,1)}, f32[320,1024]{1,0:T(8,128)}) custom-call(s32[2,16]{1,0:T(2,128)} %bitcast.20, bf16[256,640]{1,0:T(8,128)(2,1)} %bitcast.15, s32[1,256]{1,0:T(1,128)} %adv.1, bf16[320,1024]{1,0:T(8,128)(2,1)} %w.1, bf16[256,128]{1,0:T(8,128)(2,1)} %bitcast.16, bf16[256,128]{1,0:T(8,128)(2,1)} %bitcast.17, ...), custom_call_target="tpu_custom_call" | custom-call | tf_op jit(solution)/shard_map/whole/pallas_call | solution.py:618
  101.1 2.9 %finish.1 = (bf16[256,1024]{1,0:T(8,128)(2,1)}, bf16[256,128]{1,0:T(8,128)(2,1)}, bf16[256,128]{1,0:T(8,128)(2,1)}, bf16[256,128]{1,0:T(8,128)(2,1)}, bf16[256,128]{1,0:T(8,128)(2,1)}, /*index=5*/f32[320,1024]{1,0:T(8,128)}) custom-call(bf16[256,1024]{1,0:T(8,128)(2,1)} %get-tuple-element.15.dq, bf16[4,256,128]{2,1,0:T(8,128)(2,1)} %get-tuple-element.16.kv, ...), custom_call_target="tpu_custom_call" | custom-call | tf_op jit(solution)/shard_map/finish/pallas_call | solution.py:670

commit v10 on v8

--- a/solution.py
+++ b/solution.py
@@ -525,11 +525,11 @@
             segt[y, k, :, own_cols] += accs[s, k, :, 2 * SEG:]
     rring.send(0, segt[(y + 2) % 4])
     rring.send(3, segt[(y + 3) % 4])
+
+    prefix((y + 2) % 4)
+    rring.send(1, acc[...])
     gring.add_send(4, gnear[0])
     gring.add_send(5, gnear[1])
-
-    prefix((y + 2) % 4)
-    rring.send(1, acc[...])
     prefix((y + 1) % 4)
     rring.send(2, acc[...])
     rring.add_send(4, segt[(y + 1) % 4])

time: 104 us -> 102 us (0.981)
  the two profiles are of different devices: /device:TPU:34 before, /device:TPU:0 now
where the time goes in v10:
time: 102 us; the launch traced here: 101 us
  Pallas kernels  101 us (99%)
    pallas_call x1, Pallas kernels, on_device(): pl.pallas_call(whole_kernel, out_shape=(sds((TOKL, NCOL), BF), sds((4, 25...  97.8 us
    pallas_call x1, Pallas kernels, on_device(): pl.pallas_call(finish_kernel, out_shape=tuple([sds((TOKL, NCOL), BF)] + [...  2.89 us

profile of v10, /device:TPU:0, one launch (start us, length us, event | category | flops | bytes accessed | tf_op | source)
XLA Modules:
  0.0 101.3 jit_solution(14471967657675926179)
XLA Ops:
  0.6 97.8 %whole.1 = (bf16[256,1024]{1,0:T(8,128)(2,1)}, bf16[4,256,128]{2,1,0:T(8,128)(2,1)}, f32[320,1024]{1,0:T(8,128)}) custom-call(s32[2,16]{1,0:T(2,128)} %bitcast.20, bf16[256,640]{1,0:T(8,128)(2,1)} %bitcast.15, s32[1,256]{1,0:T(1,128)} %adv.1, bf16[320,1024]{1,0:T(8,128)(2,1)} %w.1, bf16[256,128]{1,0:T(8,128)(2,1)} %bitcast.16, bf16[256,128]{1,0:T(8,128)(2,1)} %bitcast.17, ...), custom_call_target="tpu_custom_call" | custom-call | tf_op jit(solution)/shard_map/whole/pallas_call | solution.py:608
  98.4 2.9 %finish.1 = (bf16[256,1024]{1,0:T(8,128)(2,1)}, bf16[256,128]{1,0:T(8,128)(2,1)}, bf16[256,128]{1,0:T(8,128)(2,1)}, bf16[256,128]{1,0:T(8,128)(2,1)}, bf16[256,128]{1,0:T(8,128)(2,1)}, /*index=5*/f32[320,1024]{1,0:T(8,128)}) custom-call(bf16[256,1024]{1,0:T(8,128)(2,1)} %get-tuple-element.15.dq, bf16[4,256,128]{2,1,0:T(8,128)(2,1)} %get-tuple-element.16.kv, ...), custom_call_target="tpu_custom_call" | custom-call | tf_op jit(solution)/shard_map/finish/pallas_call | solution.py:660
